TPU v7x, 128 devices: a whole 4x4x4 slice. The times are simulated.
128 devices in a mesh: gx: 16 (over x, y), gy: 8 (over z, core).
Axes of the slice: x: 4, y: 4, z: 4, core: 2. Of those that a mesh axis runs over, the one named last changes fastest.
Arguments:
- fractions: float32 [16, 8, 3, 1024], P('gx', 'gy'), may hold values from 0 to 1
- velocity: float32 [16, 8, 3, 1024], P('gx', 'gy'), may hold values from -4 to 4
- drag_rate: float32 [16, 8, 1024], P('gx', 'gy'), may hold values from 0.5 to 4
- volume: float32 [16, 8, 1024], P('gx', 'gy'), may hold values from 0.25 to 1
- owner: int32 [16, 8, 1024, 1], P('gx', 'gy'), may hold values from 0 to 127, as said below
- element: int32 [16, 8, 1024], P('gx', 'gy'), may hold values from 0 to 31
- coords: int32 [16, 8, 3, 1024], P('gx', 'gy'), may hold values from 0 to 63
- fluid: bfloat16 [16, 8, 32, 6, 512], P('gx', 'gy'), may hold values from -4 to 4
Outputs:
- particle_force: float32 [16, 8, 3, 1024], P('gx', 'gy')
- bin_field: float32 [4, 256, 128, 512], P(None, 'gx', 'gy')
Inputs may be any that keep to these rules, and one draw needn't show every extreme that they name: owner names a device as its gx index times the number of gy indices plus its gy index: the particle's own device or one whose gx and gy indices each differ from it by at most one (no wrap). A particle owned by a device with gx index one lower has first fraction below 0.2, one higher at least 0.8, the same gx index from 0.2 to 0.8; likewise for gy and the second fraction. Among one device's 1024 particles at most 64 have any one other device as owner, and in every device exactly 64 have one of them.
All inputs are finite; a program needn't handle non-finite values.
Results may differ from a plain program's by a relative error of at most 0.00099.
Values may be sent and summed in bfloat16 or wider, within the bound.
A program may use at most 64 MiB of HBM per device.

v0:
```python
import jax
import jax.numpy as jnp
import numpy as np
from jax import lax
from jax.sharding import PartitionSpec as P

P_DEV = 1024
E_DEV = 32
BINS_THIRD_AXIS = 512
BX = 16
BY = 16
MARGIN = 4
QUANT = 64
CAP = 64


GLL_NODES = (
    -1.0,
    -0.8717401485096066,
    -0.5917001814331423,
    -0.2092992179024789,
    0.2092992179024789,
    0.5917001814331423,
    0.8717401485096066,
    1.0,
)
STIFFNESS = 0.5
PAIR_WIDTH = 0.3
FILTER_BINS = 3.0


def padded(block, sides, width):
    for axis, dim in sides:
        count = lax.axis_size(axis)
        forward = [(i, i + 1) for i in range(count - 1)]
        backward = [(target, source) for source, target in forward]
        low = lax.ppermute(
            lax.slice_in_dim(block, block.shape[dim] - width, None, axis=dim), axis, forward
        )
        high = lax.ppermute(lax.slice_in_dim(block, 0, width, axis=dim), axis, backward)
        block = jnp.concatenate([low, block, high], axis=dim)
    return block


def basis_table(levels):
    points = -1.0 + (2.0 * np.arange(levels) + 1.0) / levels
    lagrange = np.ones((levels, 8))
    for node_a in range(8):
        for node_b in range(8):
            if node_b != node_a:
                lagrange[:, node_a] *= (points - GLL_NODES[node_b]) / (
                    GLL_NODES[node_a] - GLL_NODES[node_b]
                )
    return jnp.asarray(lagrange, dtype=jnp.float32)


def place(fractions, slab_x, slab_y):
    return jnp.stack(
        [slab_x + fractions[0], slab_y + fractions[1], fractions[2] * (BINS_THIRD_AXIS / BX)]
    )


def gaussian_rows(along, centres, deviation):
    distance = along[:, None] - centres[None, :]
    bumps = jnp.exp(-(distance * distance) / (2.0 * deviation * deviation))
    return bumps / jnp.sum(bumps, axis=1, keepdims=True)


def window_cube(positions, loads, slab_x, slab_y, span_x, span_y):
    first_extent = BX + 2 * MARGIN
    second_extent = BY + 2 * MARGIN
    centre_x = slab_x + (jnp.arange(first_extent, dtype=jnp.float32) - MARGIN + 0.5) / BX
    centre_y = slab_y + (jnp.arange(second_extent, dtype=jnp.float32) - MARGIN + 0.5) / BY
    centre_z = (jnp.arange(BINS_THIRD_AXIS, dtype=jnp.float32) + 0.5) / BX
    along_x = gaussian_rows(positions[0], centre_x, FILTER_BINS / BX)[
        :, span_x[0] : span_x[0] + span_x[1]
    ]
    along_y = gaussian_rows(positions[1], centre_y, FILTER_BINS / BY)[
        :, span_y[0] : span_y[0] + span_y[1]
    ]
    along_depth = gaussian_rows(positions[2], centre_z, FILTER_BINS / BX).astype(jnp.bfloat16)
    plane = (along_x[:, :, None] * along_y[:, None, :]).reshape(
        positions.shape[1], span_x[1] * span_y[1]
    )
    scattered_loads = (loads[:, :, None] * plane[None, :, :]).astype(jnp.bfloat16)
    filter_cube = jnp.einsum(
        "vtn,tl->vnl", scattered_loads, along_depth, preferred_element_type=jnp.float32
    )
    return filter_cube.reshape(4, span_x[1], span_y[1], BINS_THIRD_AXIS)


def pair_forces(own, blocks, present):
    particles = own.shape[1]
    row_count = min(512, particles)
    groups = particles // row_count
    stacked = own.reshape(3, groups, row_count).transpose(1, 0, 2)

    def one_group(subset):
        summed = jnp.zeros((3, row_count), own.dtype)
        for ghost_block, weight in zip(blocks, present):
            offset = subset[:, :, None] - ghost_block[:, None, :]
            closeness = (
                jnp.exp(-jnp.sum(offset * offset, axis=0) / (2.0 * PAIR_WIDTH * PAIR_WIDTH))
                * weight
            )
            summed = summed + jnp.sum(offset * closeness[None, :, :], axis=2)
        return summed

    return STIFFNESS * lax.map(one_group, stacked).transpose(1, 0, 2).reshape(3, particles)


def interpolate_slots(flat, fluid, lagrange):
    slots = flat.shape[1]
    levels = jnp.arange(QUANT, dtype=jnp.int32)
    factors = []
    for column in range(3):
        select = (flat[1 + column][None, :] == levels[:, None]).astype(jnp.float32)
        factors.append(
            jnp.dot(
                lagrange.T,
                select,
                precision=lax.Precision.HIGHEST,
                preferred_element_type=jnp.float32,
            )
        )
    weights = (
        (factors[0][:, None, None, :] * factors[1][None, :, None, :] * factors[2][None, None, :, :])
        .reshape(512, slots)
        .astype(jnp.bfloat16)
    )
    table = fluid.reshape(E_DEV * 6, 512)
    projected = jnp.dot(table, weights, preferred_element_type=jnp.float32).reshape(E_DEV, 6, slots)
    picked = (flat[0][None, :] == jnp.arange(E_DEV, dtype=jnp.int32)[:, None]).astype(jnp.float32)
    values = jnp.sum(projected * picked[:, None, :], axis=0)
    return values.astype(jnp.bfloat16)


def flatten_blocks(blocks):
    return blocks.transpose(2, 0, 1, 3).reshape(blocks.shape[2], 9 * CAP)


def unflatten_blocks(values):
    return values.reshape(values.shape[0], 3, 3, CAP).transpose(1, 2, 0, 3)


def margin_spans(inner):
    return ((-1, inner + MARGIN, 0, MARGIN), (0, MARGIN, 0, inner), (1, 0, inner - MARGIN, MARGIN))


def body(fractions, velocity, drag_rate, volume, owner, element, coords, fluid):
    grid_x = lax.axis_size("gx")
    grid_y = lax.axis_size("gy")
    index_x = lax.axis_index("gx")
    index_y = lax.axis_index("gy")
    slab_x = index_x.astype(jnp.float32)
    slab_y = index_y.astype(jnp.float32)
    lagrange = basis_table(QUANT)
    targets = owner.reshape(P_DEV)
    step_x = targets // grid_y - index_x
    step_y = targets % grid_y - index_y
    code = (step_x + 1) * 3 + step_y + 1
    remote = code != 4
    chosen = (code[:, None] == jnp.arange(9, dtype=jnp.int32)[None, :]).astype(jnp.bfloat16)
    order = jnp.arange(P_DEV, dtype=jnp.int32)
    earlier = (order[None, :] < order[:, None]).astype(jnp.bfloat16)
    ranks = jnp.dot(earlier, chosen, preferred_element_type=jnp.float32)
    slot = jnp.sum(ranks * chosen.astype(jnp.float32), axis=1).astype(jnp.int32)
    position_index = jnp.where(remote, code * CAP + slot, 9 * CAP)
    payload = jnp.concatenate([element.reshape(1, P_DEV), coords.reshape(3, P_DEV)], axis=0)
    outgoing = (
        jnp.zeros((4, 9 * CAP + 1), jnp.int32).at[:, position_index].set(payload)[:, : 9 * CAP]
    )
    outgoing = outgoing.reshape(4, 3, 3, CAP).transpose(1, 2, 0, 3)
    own_values = interpolate_slots(payload, fluid, lagrange)
    arrived = padded(outgoing, (("gx", 0), ("gy", 1)), 1)[::2, ::2]
    served = unflatten_blocks(interpolate_slots(flatten_blocks(arrived), fluid, lagrange))
    returned = padded(served, (("gx", 0), ("gy", 1)), 1)[::2, ::2]
    remote_values = flatten_blocks(returned)[:, jnp.minimum(position_index, 9 * CAP - 1)]
    fetched = jnp.where(remote[None, :], remote_values, own_values).astype(jnp.float32)
    ghosts = padded(fractions, (("gx", 0), ("gy", 1)), 1)
    blocks = []
    present = []
    for shift_x in (-1, 0, 1):
        for shift_y in (-1, 0, 1):
            blocks.append(
                place(ghosts[1 + shift_x, 1 + shift_y], slab_x + shift_x, slab_y + shift_y)
            )
            inside = (
                (index_x + shift_x >= 0)
                & (index_x + shift_x < grid_x)
                & (index_y + shift_y >= 0)
                & (index_y + shift_y < grid_y)
            )
            present.append(inside.astype(jnp.float32))
    own = place(fractions[0, 0], slab_x, slab_y)
    pair = pair_forces(own, blocks, present)
    force = (
        drag_rate.reshape(1, P_DEV) * (fetched[0:3] - velocity[0, 0])
        - volume.reshape(1, P_DEV) * fetched[3:6]
        + pair
    )
    loads = jnp.concatenate([force, volume.reshape(1, P_DEV)], axis=0)
    field = jnp.zeros((4, BX, BY, BINS_THIRD_AXIS), jnp.float32)
    ghost_loads = padded(loads.reshape(1, 1, 4, P_DEV), (("gx", 0), ("gy", 1)), 1)
    for shift_x, source_x, target_x, length_x in margin_spans(BX):
        for shift_y, source_y, target_y, length_y in margin_spans(BY):
            piece = window_cube(
                blocks[3 * (shift_x + 1) + shift_y + 1],
                ghost_loads[1 + shift_x, 1 + shift_y],
                slab_x + shift_x,
                slab_y + shift_y,
                (source_x, length_x),
                (source_y, length_y),
            )
            field = field.at[:, target_x : target_x + length_x, target_y : target_y + length_y].add(
                piece
            )
    bin_field = field * (BX * BY * BINS_THIRD_AXIS / P_DEV)
    return (force.reshape(1, 1, 3, P_DEV), bin_field)


def solution(mesh):
    return jax.shard_map(
        body,
        mesh=mesh,
        in_specs=(
            P("gx", "gy", None, None),
            P("gx", "gy", None, None),
            P("gx", "gy", None),
            P("gx", "gy", None),
            P("gx", "gy", None, None),
            P("gx", "gy", None),
            P("gx", "gy", None, None),
            P("gx", "gy", None, None, None),
        ),
        out_specs=(P("gx", "gy", None, None), P(None, "gx", "gy", None)),
        check_vma=False,
    )
```

profile of v0, /device:TPU:7, one launch (start us, length us, event | category | flops | bytes accessed | tf_op | source)
XLA Modules:
  0.0 147.4 jit_solution(10589177698586059885)
XLA Ops:
  0.7 3.3 %collective-permute-start.8 = (f32[1,1,3,1024]{3,1,2,0:T(1,128)}, f32[1,1,3,1024]{3,1,2,0:T(1,128)S(1)}, u32[]{:S(2)}, u32[]{:S(2)}) collective-permute-start(f32[1,1,3,1024]{3,1,2,0:T(1,128)} %param.31), channel_id=1, source_target_pairs={{0,8},{8,16},{16,24},{24,32},{32,40},{40,48},{48,56},{56,64},{64,7... | collective-permute-start | bytes 36872 | tf_op jit(solution)/shard_map/ppermute | solution.py:37
  4.0 4.2 %collective-permute-start.9 = (f32[1,1,3,1024]{3,1,2,0:T(1,128)}, f32[1,1,3,1024]{3,1,2,0:T(1,128)S(1)}, u32[]{:S(2)}, u32[]{:S(2)}) collective-permute-start(f32[1,1,3,1024]{3,1,2,0:T(1,128)} %param.31), channel_id=1, source_target_pairs={{8,0},{16,8},{24,16},{32,24},{40,32},{48,40},{56,48},{64,56},{72,6... | collective-permute-start | bytes 36872 | tf_op jit(solution)/shard_map/ppermute | solution.py:40
  11.8 3.1 %scatter_custom_fusion = s32[4,577]{0,1:T(8,128)S(1)} fusion(s32[1024]{0:T(1024)S(1)} %bitcast.292, s32[1024,4]{1,0:T(8,128)S(1)} %copy.50, s32[]{:T(128)} %constant.365.clone.1), kind=kCustom, calls=%fused_computation.173 | custom fusion | bytes 9236 | tf_op jit(solution)/shard_map/scatter | solution.py:171
  15.2 1.9 %collective-permute-start = (s32[1,3,4,64]{3,1,0,2:T(4,128)S(1)}, s32[1,3,4,64]{3,1,0,2:T(4,128)S(1)}, u32[]{:S(2)}, u32[]{:S(2)}) collective-permute-start(s32[1,3,4,64]{3,1,0,2:T(4,128)S(1)} %get-tuple-element.371), channel_id=1, source_target_pairs={{0,8},{8,16},{16,24},{24,32},{32,40},{40,48},{48,56},{56,64},{64,7... | collective-permute-start | bytes 9224 | tf_op jit(solution)/shard_map/ppermute | solution.py:37
  17.1 5.5 %collective-permute-start.1 = (s32[1,3,4,64]{3,1,0,2:T(4,128)S(1)}, s32[1,3,4,64]{3,1,0,2:T(4,128)S(1)}, u32[]{:S(2)}, u32[]{:S(2)}) collective-permute-start(s32[1,3,4,64]{3,1,0,2:T(4,128)S(1)} %get-tuple-element.372), channel_id=1, source_target_pairs={{8,0},{16,8},{24,16},{32,24},{40,32},{48,40},{56,48},{64,56},{72,6... | collective-permute-start | bytes 9224 | tf_op jit(solution)/shard_map/ppermute | solution.py:40
  26.2 5.2 %collective-permute-start.2 = (s32[5,1,4,64]{3,1,0,2:T(1,128)S(1)}, s32[5,1,4,64]{3,1,0,2:T(1,128)S(1)}, u32[]{:S(2)}, u32[]{:S(2)}) collective-permute-start(s32[5,1,4,64]{3,1,0,2:T(1,128)S(1)} %get-tuple-element.339), channel_id=1, source_target_pairs={{0,1},{1,2},{2,3},{3,4},{4,5},{5,6},{6,7},{8,9},{9,10},{10,11},{11... | collective-permute-start | bytes 15368 | tf_op jit(solution)/shard_map/ppermute | solution.py:37
  31.4 1.9 %collective-permute-start.3 = (s32[5,1,4,64]{3,1,0,2:T(1,128)S(1)}, s32[5,1,4,64]{3,1,0,2:T(1,128)S(1)}, u32[]{:S(2)}, u32[]{:S(2)}) collective-permute-start(s32[5,1,4,64]{3,1,0,2:T(1,128)S(1)} %get-tuple-element.340), channel_id=1, source_target_pairs={{1,0},{2,1},{3,2},{4,3},{5,4},{6,5},{7,6},{9,8},{10,9},{11,10},{12... | collective-permute-start | bytes 15368 | tf_op jit(solution)/shard_map/ppermute | solution.py:40
  33.4 3.0 %collective-permute-done.3 = s32[5,1,4,64]{3,1,0,2:T(1,128)S(1)} collective-permute-done((s32[5,1,4,64]{3,1,0,2:T(1,128)S(1)}, s32[5,1,4,64]{3,1,0,2:T(1,128)S(1)}, u32[]{:S(2)}, u32[]{:S(2)}) %collective-permute-start.3) | collective-permute-done | bytes 5152 | tf_op jit(solution)/shard_map/ppermute | solution.py:40
  40.6 5.5 %collective-permute-start.5 = (bf16[1,3,6,64]{3,2,1,0:T(8,128)(2,1)S(1)}, bf16[1,3,6,64]{3,2,1,0:T(8,128)(2,1)S(1)}, u32[]{:S(2)}, u32[]{:S(2)}) collective-permute-start(bf16[1,3,6,64]{3,2,1,0:T(8,128)(2,1)S(1)} %get-tuple-element.374), channel_id=1, source_target_pairs={{8,0},{16,8},{24,16},{32,24},{40,32},{48,40},{56,48},{64,56},{72,6... | collective-permute-start | bytes 6920 | tf_op jit(solution)/shard_map/ppermute | solution.py:40
  46.9 3.1 %collective-permute-start.6 = (bf16[5,1,6,64]{3,2,1,0:T(8,128)(2,1)S(1)}, bf16[5,1,6,64]{3,2,1,0:T(8,128)(2,1)S(1)}, u32[]{:S(2)}, u32[]{:S(2)}) collective-permute-start(bf16[5,1,6,64]{3,2,1,0:T(8,128)(2,1)S(1)} %get-tuple-element.365), channel_id=1, source_target_pairs={{0,1},{1,2},{2,3},{3,4},{4,5},{5,6},{6,7},{8,9},{9,10},{10,11},{11... | collective-permute-start | bytes 11528 | tf_op jit(solution)/shard_map/ppermute | solution.py:37
  51.9 3.6 %collective-permute-start.10 = (f32[3,1,3,1024]{3,1,2,0:T(1,128)S(1)}, f32[3,1,3,1024]{3,1,2,0:T(1,128)S(1)}, u32[]{:S(2)}, u32[]{:S(2)}) collective-permute-start(f32[3,1,3,1024]{3,1,2,0:T(1,128)S(1)} %constant_dynamic-update-slice_fusion), channel_id=1, source_target_pairs={{0,1},{1,2},{2,3},{3,4},{4,5},{5,6},{6,7},{8,9},{9,10},{10,11},{11... | collective-permute-start | bytes 110600 | tf_op jit(solution)/shard_map/ppermute | solution.py:37
  55.6 2.1 %collective-permute-start.11 = (f32[3,1,3,1024]{3,1,2,0:T(1,128)S(1)}, f32[3,1,3,1024]{3,1,2,0:T(1,128)S(1)}, u32[]{:S(2)}, u32[]{:S(2)}) collective-permute-start(f32[3,1,3,1024]{3,1,2,0:T(1,128)S(1)} %constant_dynamic-update-slice_fusion), channel_id=1, source_target_pairs={{1,0},{2,1},{3,2},{4,3},{5,4},{6,5},{7,6},{9,8},{10,9},{11,10},{12... | collective-permute-start | bytes 110600 | tf_op jit(solution)/shard_map/ppermute | solution.py:40
  58.2 3.2 %gather_fusion = bf16[1024,6]{1,0:T(8,128)(2,1)S(1)} fusion(bf16[6,576]{0,1:T(8,128)(2,1)S(1)} %bitcast.212, s32[1024]{0:T(1024)S(1)} %broadcast_clamp_fusion), kind=kCustom, calls=%fused_computation | custom fusion | bytes 28672 | tf_op jit(solution)/shard_map/gather | solution.py:178
  61.9 37.9 %while.20 = (s32[]{:T(128)}, f32[2,3,512]{2,1,0:T(4,128)S(1)}, f32[2,3,512]{2,1,0:T(4,128)S(1)}, f32[3,1024]{1,0:T(4,128)S(1)}, f32[]{:T(128)}, /*index=5*/f32[3...) while((s32[]{:T(128)}, f32[2,3,512]{2,1,0:T(4,128)S(1)}, ...), condition=%wide.region_23.24_spmd, body=%wide.region_4.23_spmd.sunk | while | flops 94370304 | bytes 75886824 | solution.py:109
  64.5 7.9 %fusion.193 = (f32[3,512]{1,0:T(4,128)S(1)}, f32[512,1024]{1,0:T(8,128)S(1)}, f32[512,1024]{1,0:T(8,128)S(1)}, f32[512,1024]{1,0:T(8,128)S(1)}, f32[512,1024]{1,...) fusion(f32[512,1024]{1,0:T(8,128)S(1)} %exponential_multiply_fu, ...), kind=kLoop, calls=%fused_computation.23.clone.1 | loop fusion | flops 38794240 | bytes 19003392 | tf_op jit(solution)/shard_map/while/body/eval_jaxpr/reduce_sum | solution.py:106
  75.8 5.1 %fusion.194 = (f32[3,512]{1,0:T(4,128)S(1)}, f32[3,512]{1,0:T(4,128)S(1)}, f32[3,512]{1,0:T(4,128)S(1)}, f32[3,512]{1,0:T(4,128)S(1)}, f32[3,512]{1,0:T(4,128)S(...) fusion(f32[512,1024]{1,0:T(8,128)S(1)} %exponential_multiply_fusion.17, f32[3,1024]{1,0:T(4,128)S(1)} %get-tuple-element.658, ...), kind=kLoop, calls=%fused_computation.25.clone.1 | loop fusion | flops 33019392 | bytes 14815232 | tf_op jit(solution)/shard_map/while/body/eval_jaxpr/reduce_sum | solution.py:106
  83.4 7.9 %fusion.193 = (f32[3,512]{1,0:T(4,128)S(1)}, f32[512,1024]{1,0:T(8,128)S(1)}, f32[512,1024]{1,0:T(8,128)S(1)}, f32[512,1024]{1,0:T(8,128)S(1)}, f32[512,1024]{1,...) fusion(f32[512,1024]{1,0:T(8,128)S(1)} %exponential_multiply_fu, ...), kind=kLoop, calls=%fused_computation.23.clone.1 | loop fusion | flops 38794240 | bytes 19003392 | tf_op jit(solution)/shard_map/while/body/eval_jaxpr/reduce_sum | solution.py:106
  94.7 5.1 %fusion.194 = (f32[3,512]{1,0:T(4,128)S(1)}, f32[3,512]{1,0:T(4,128)S(1)}, f32[3,512]{1,0:T(4,128)S(1)}, f32[3,512]{1,0:T(4,128)S(1)}, f32[3,512]{1,0:T(4,128)S(...) fusion(f32[512,1024]{1,0:T(8,128)S(1)} %exponential_multiply_fusion.17, f32[3,1024]{1,0:T(4,128)S(1)} %get-tuple-element.658, ...), kind=kLoop, calls=%fused_computation.25.clone.1 | loop fusion | flops 33019392 | bytes 14815232 | tf_op jit(solution)/shard_map/while/body/eval_jaxpr/reduce_sum | solution.py:106
  102.7 6.2 %collective-permute-start.13 = (f32[1,1,4,1024]{3,2,1,0:T(4,128)S(1)}, f32[1,1,4,1024]{3,2,1,0:T(4,128)S(1)}, u32[]{:S(2)}, u32[]{:S(2)}) collective-permute-start(f32[1,1,4,1024]{3,2,1,0:T(4,128)S(1)} %fusion.188), channel_id=1, source_target_pairs={{8,0},{16,8},{24,16},{32,24},{40,32},{48,40},{56,48},{64,56},{72,6... | collective-permute-start | bytes 49160 | tf_op jit(solution)/shard_map/ppermute | solution.py:40
  110.4 5.2 %fusion.20 = (f32[1024]{0:T(1024)}, f32[1024]{0:T(1024)S(1)}, f32[1024]{0:T(1024)S(1)}, f32[1024]{0:T(1024)S(1)}, f32[1024]{0:T(1024)S(1)}, /*index=5*/f32[1024]...) fusion(f32[1024]{0:T(1024)S(1)} %bitcast.280, f32[512]{0:T(512)S(1)} %add_multiply_fusion, ...), kind=kLoop, calls=%fused_computation.55 | loop fusion | flops 23583744 | bytes 75776 | tf_op jit(solution)/shard_map/reduce_sum | solution.py:66
  115.6 2.7 %fusion.19 = f32[4,256,512]{2,1,0:T(8,128)} fusion(f32[1024,256]{0,1:T(8,128)S(1)} %bitcast.211, f32[4,1024]{1,0:T(4,128)S(1)} %pad_maximum_fusion.11, f32[1024]{0:T(1024)S(1)} %get-tuple-element.256, f32[1024]{0:T(1024)S(1)} %bitcast.278, f32[512]{0:T(512)S(1)} %add_multiply_fusion), kind=kOutput, calls=%fused_computation.52 | convolution fusion | flops 1078984704 | bytes 3172352 | tf_op jit(solution)/shard_map/vtn,tl->vnl/dot_general | solution.py:86
  120.8 3.9 %collective-permute-start.14 = (f32[3,1,4,1024]{3,2,1,0:T(4,128)S(1)}, f32[3,1,4,1024]{3,2,1,0:T(4,128)S(1)}, u32[]{:S(2)}, u32[]{:S(2)}) collective-permute-start(f32[3,1,4,1024]{3,2,1,0:T(4,128)S(1)} %pad_maximum_fusion.1), channel_id=1, source_target_pairs={{0,1},{1,2},{2,3},{3,4},{4,5},{5,6},{6,7},{8,9},{9,10},{10,11},{11... | collective-permute-start | bytes 147464 | tf_op jit(solution)/shard_map/ppermute | solution.py:37
  136.2 2.5 %fusion.45 = f32[4,64,512]{2,1,0:T(8,128)} fusion(f32[1024]{0:T(1024)S(1)} %copy-done.19, f32[1024]{0:T(1024)S(1)} %bitcast.283, f32[512]{0:T(512)S(1)} %copy-done.16, f32[1024,64]{0,1:T(8,128)} %mul.1066, f32[4,1024]{1,0:T(4,128)S(1)} %get-tuple-element.334), kind=kOutput, calls=%fused_computation.98 | convolution fusion | flops 272105472 | bytes 813056 | tf_op jit(solution)/shard_map/vtn,tl->vnl/dot_general | solution.py:86
  142.5 2.1 %add.1056 = f32[4,16,16,512]{3,2,1,0:T(8,128)S(1)} add(f32[4,16,16,512]{3,2,1,0:T(8,128)S(1)} %fusion.82, f32[4,16,16,512]{3,2,1,0:T(8,128)} %bitcast.209) | non-fusion elementwise | flops 524288 | bytes 6291456 | tf_op jit(solution)/shard_map/add | solution.py:215
  (218 shorter events, 50.9 us)
Async XLA Ops:
  0.6 22.3 %copy-start = (f32[64,8]{1,0:T(8,128)S(1)}, f32[64,8]{1,0:T(8,128)}, u32[]{:S(2)}) copy-start(f32[64,8]{1,0:T(8,128)} %constant.392.clone) | copy-start | bytes 6148
  0.7 22.1 %copy-start.2 = (bf16[1,1,32,6,512]{4,2,3,1,0:T(8,128)(2,1)S(1)}, bf16[1,1,32,6,512]{4,2,3,1,0:T(8,128)(2,1)}, u32[]{:S(2)}) copy-start(bf16[1,1,32,6,512]{4,2,3,1,0:T(8,128)(2,1)} %param.38) | copy-start | bytes 589828
  0.7 51.2 %collective-permute-start.8 = (f32[1,1,3,1024]{3,1,2,0:T(1,128)}, f32[1,1,3,1024]{3,1,2,0:T(1,128)S(1)}, u32[]{:S(2)}, u32[]{:S(2)}) collective-permute-start(f32[1,1,3,1024]{3,1,2,0:T(1,128)} %param.31), channel_id=1, source_target_pairs={{0,8},{8,16},{16,24},{24,32},{32,40},{40,48},{48,56},{56,64},{64,7... | collective-permute-start | bytes 36872 | tf_op jit(solution)/shard_map/ppermute | solution.py:37
  4.0 47.9 %collective-permute-start.9 = (f32[1,1,3,1024]{3,1,2,0:T(1,128)}, f32[1,1,3,1024]{3,1,2,0:T(1,128)S(1)}, u32[]{:S(2)}, u32[]{:S(2)}) collective-permute-start(f32[1,1,3,1024]{3,1,2,0:T(1,128)} %param.31), channel_id=1, source_target_pairs={{8,0},{16,8},{24,16},{32,24},{40,32},{48,40},{56,48},{64,56},{72,6... | collective-permute-start | bytes 36872 | tf_op jit(solution)/shard_map/ppermute | solution.py:40
  15.2 11.0 %collective-permute-start = (s32[1,3,4,64]{3,1,0,2:T(4,128)S(1)}, s32[1,3,4,64]{3,1,0,2:T(4,128)S(1)}, u32[]{:S(2)}, u32[]{:S(2)}) collective-permute-start(s32[1,3,4,64]{3,1,0,2:T(4,128)S(1)} %get-tuple-element.371), channel_id=1, source_target_pairs={{0,8},{8,16},{16,24},{24,32},{32,40},{40,48},{48,56},{56,64},{64,7... | collective-permute-start | bytes 9224 | tf_op jit(solution)/shard_map/ppermute | solution.py:37
  17.1 9.1 %collective-permute-start.1 = (s32[1,3,4,64]{3,1,0,2:T(4,128)S(1)}, s32[1,3,4,64]{3,1,0,2:T(4,128)S(1)}, u32[]{:S(2)}, u32[]{:S(2)}) collective-permute-start(s32[1,3,4,64]{3,1,0,2:T(4,128)S(1)} %get-tuple-element.372), channel_id=1, source_target_pairs={{8,0},{16,8},{24,16},{32,24},{40,32},{48,40},{56,48},{64,56},{72,6... | collective-permute-start | bytes 9224 | tf_op jit(solution)/shard_map/ppermute | solution.py:40
  22.7 106.3 %copy-start.14 = (f32[512]{0:T(512)}, f32[512]{0:T(512)S(1)}, u32[]{:S(2)}) copy-start(f32[512]{0:T(512)S(1)} %add_multiply_fusion) | copy-start | bytes 6148
  26.2 7.2 %collective-permute-start.2 = (s32[5,1,4,64]{3,1,0,2:T(1,128)S(1)}, s32[5,1,4,64]{3,1,0,2:T(1,128)S(1)}, u32[]{:S(2)}, u32[]{:S(2)}) collective-permute-start(s32[5,1,4,64]{3,1,0,2:T(1,128)S(1)} %get-tuple-element.339), channel_id=1, source_target_pairs={{0,1},{1,2},{2,3},{3,4},{4,5},{5,6},{6,7},{8,9},{9,10},{10,11},{11... | collective-permute-start | bytes 15368 | tf_op jit(solution)/shard_map/ppermute | solution.py:37
  31.4 5.0 %collective-permute-start.3 = (s32[5,1,4,64]{3,1,0,2:T(1,128)S(1)}, s32[5,1,4,64]{3,1,0,2:T(1,128)S(1)}, u32[]{:S(2)}, u32[]{:S(2)}) collective-permute-start(s32[5,1,4,64]{3,1,0,2:T(1,128)S(1)} %get-tuple-element.340), channel_id=1, source_target_pairs={{1,0},{2,1},{3,2},{4,3},{5,4},{6,5},{7,6},{9,8},{10,9},{11,10},{12... | collective-permute-start | bytes 15368 | tf_op jit(solution)/shard_map/ppermute | solution.py:40
  38.7 7.9 %collective-permute-start.4 = (bf16[1,3,6,64]{3,2,1,0:T(8,128)(2,1)S(1)}, bf16[1,3,6,64]{3,2,1,0:T(8,128)(2,1)S(1)}, u32[]{:S(2)}, u32[]{:S(2)}) collective-permute-start(bf16[1,3,6,64]{3,2,1,0:T(8,128)(2,1)S(1)} %get-tuple-element.373), channel_id=1, source_target_pairs={{0,8},{8,16},{16,24},{24,32},{32,40},{40,48},{48,56},{56,64},{64,7... | collective-permute-start | bytes 6920 | tf_op jit(solution)/shard_map/ppermute | solution.py:37
  40.6 6.2 %collective-permute-start.5 = (bf16[1,3,6,64]{3,2,1,0:T(8,128)(2,1)S(1)}, bf16[1,3,6,64]{3,2,1,0:T(8,128)(2,1)S(1)}, u32[]{:S(2)}, u32[]{:S(2)}) collective-permute-start(bf16[1,3,6,64]{3,2,1,0:T(8,128)(2,1)S(1)} %get-tuple-element.374), channel_id=1, source_target_pairs={{8,0},{16,8},{24,16},{32,24},{40,32},{48,40},{56,48},{64,56},{72,6... | collective-permute-start | bytes 6920 | tf_op jit(solution)/shard_map/ppermute | solution.py:40
  46.9 11.1 %collective-permute-start.6 = (bf16[5,1,6,64]{3,2,1,0:T(8,128)(2,1)S(1)}, bf16[5,1,6,64]{3,2,1,0:T(8,128)(2,1)S(1)}, u32[]{:S(2)}, u32[]{:S(2)}) collective-permute-start(bf16[5,1,6,64]{3,2,1,0:T(8,128)(2,1)S(1)} %get-tuple-element.365), channel_id=1, source_target_pairs={{0,1},{1,2},{2,3},{3,4},{4,5},{5,6},{6,7},{8,9},{9,10},{10,11},{11... | collective-permute-start | bytes 11528 | tf_op jit(solution)/shard_map/ppermute | solution.py:37
  49.9 8.0 %collective-permute-start.7 = (bf16[5,1,6,64]{3,2,1,0:T(8,128)(2,1)S(1)}, bf16[5,1,6,64]{3,2,1,0:T(8,128)(2,1)S(1)}, u32[]{:S(2)}, u32[]{:S(2)}) collective-permute-start(bf16[5,1,6,64]{3,2,1,0:T(8,128)(2,1)S(1)} %get-tuple-element.366), channel_id=1, source_target_pairs={{1,0},{2,1},{3,2},{4,3},{5,4},{6,5},{7,6},{9,8},{10,9},{11,10},{12... | collective-permute-start | bytes 11528 | tf_op jit(solution)/shard_map/ppermute | solution.py:40
  51.9 9.8 %collective-permute-start.10 = (f32[3,1,3,1024]{3,1,2,0:T(1,128)S(1)}, f32[3,1,3,1024]{3,1,2,0:T(1,128)S(1)}, u32[]{:S(2)}, u32[]{:S(2)}) collective-permute-start(f32[3,1,3,1024]{3,1,2,0:T(1,128)S(1)} %constant_dynamic-update-slice_fusion), channel_id=1, source_target_pairs={{0,1},{1,2},{2,3},{3,4},{4,5},{5,6},{6,7},{8,9},{9,10},{10,11},{11... | collective-permute-start | bytes 110600 | tf_op jit(solution)/shard_map/ppermute | solution.py:37
  55.6 6.1 %collective-permute-start.11 = (f32[3,1,3,1024]{3,1,2,0:T(1,128)S(1)}, f32[3,1,3,1024]{3,1,2,0:T(1,128)S(1)}, u32[]{:S(2)}, u32[]{:S(2)}) collective-permute-start(f32[3,1,3,1024]{3,1,2,0:T(1,128)S(1)} %constant_dynamic-update-slice_fusion), channel_id=1, source_target_pairs={{1,0},{2,1},{3,2},{4,3},{5,4},{6,5},{7,6},{9,8},{10,9},{11,10},{12... | collective-permute-start | bytes 110600 | tf_op jit(solution)/shard_map/ppermute | solution.py:40
  61.7 48.7 %copy-start.9 = (f32[1,1,1,1024]{3,1,2,0:T(1,128)}, f32[1,1,1,1024]{3,1,2,0:T(1,128)S(1)}, u32[]{:S(2)}) copy-start(f32[1,1,1,1024]{3,1,2,0:T(1,128)S(1)} %get-tuple-element.357) | copy-start | bytes 12292
  61.7 48.7 %copy-start.10 = (f32[1,1,1,1024]{3,1,2,0:T(1,128)}, f32[1,1,1,1024]{3,1,2,0:T(1,128)S(1)}, u32[]{:S(2)}) copy-start(f32[1,1,1,1024]{3,1,2,0:T(1,128)S(1)} %get-tuple-element.353) | copy-start | bytes 12292
  61.8 48.6 %copy-start.12 = (f32[1,1,1,1024]{3,1,2,0:T(1,128)}, f32[1,1,1,1024]{3,1,2,0:T(1,128)S(1)}, u32[]{:S(2)}) copy-start(f32[1,1,1,1024]{3,1,2,0:T(1,128)S(1)} %get-tuple-element.345) | copy-start | bytes 12292
  61.9 38.1 %copy-start.5 = (f32[1,1,1024]{2,1,0:T(1,128)S(1)}, f32[1,1,1024]{2,1,0:T(1,128)}, u32[]{:S(2)}) copy-start(f32[1,1,1024]{2,1,0:T(1,128)} %param.34) | copy-start | bytes 12292
  61.9 38.1 %copy-start.8 = (f32[1,1,1024]{2,1,0:T(1,128)S(1)}, f32[1,1,1024]{2,1,0:T(1,128)}, u32[]{:S(2)}) copy-start(f32[1,1,1024]{2,1,0:T(1,128)} %param.33) | copy-start | bytes 12292
  100.8 20.0 %collective-permute-start.12 = (f32[1,1,4,1024]{3,2,1,0:T(4,128)S(1)}, f32[1,1,4,1024]{3,2,1,0:T(4,128)S(1)}, u32[]{:S(2)}, u32[]{:S(2)}) collective-permute-start(f32[1,1,4,1024]{3,2,1,0:T(4,128)S(1)} %fusion.188), channel_id=1, source_target_pairs={{0,8},{8,16},{16,24},{24,32},{32,40},{40,48},{48,56},{56,64},{64,7... | collective-permute-start | bytes 49160 | tf_op jit(solution)/shard_map/ppermute | solution.py:37
  102.7 18.1 %collective-permute-start.13 = (f32[1,1,4,1024]{3,2,1,0:T(4,128)S(1)}, f32[1,1,4,1024]{3,2,1,0:T(4,128)S(1)}, u32[]{:S(2)}, u32[]{:S(2)}) collective-permute-start(f32[1,1,4,1024]{3,2,1,0:T(4,128)S(1)} %fusion.188), channel_id=1, source_target_pairs={{8,0},{16,8},{24,16},{32,24},{40,32},{48,40},{56,48},{64,56},{72,6... | collective-permute-start | bytes 49160 | tf_op jit(solution)/shard_map/ppermute | solution.py:40
  120.8 8.2 %collective-permute-start.14 = (f32[3,1,4,1024]{3,2,1,0:T(4,128)S(1)}, f32[3,1,4,1024]{3,2,1,0:T(4,128)S(1)}, u32[]{:S(2)}, u32[]{:S(2)}) collective-permute-start(f32[3,1,4,1024]{3,2,1,0:T(4,128)S(1)} %pad_maximum_fusion.1), channel_id=1, source_target_pairs={{0,1},{1,2},{2,3},{3,4},{4,5},{5,6},{6,7},{8,9},{9,10},{10,11},{11... | collective-permute-start | bytes 147464 | tf_op jit(solution)/shard_map/ppermute | solution.py:37
  124.7 5.4 %collective-permute-start.15 = (f32[3,1,4,1024]{3,2,1,0:T(4,128)S(1)}, f32[3,1,4,1024]{3,2,1,0:T(4,128)S(1)}, u32[]{:S(2)}, u32[]{:S(2)}) collective-permute-start(f32[3,1,4,1024]{3,2,1,0:T(4,128)S(1)} %pad_maximum_fusion.1), channel_id=1, source_target_pairs={{1,0},{2,1},{3,2},{4,3},{5,4},{6,5},{7,6},{9,8},{10,9},{11,10},{12... | collective-permute-start | bytes 147464 | tf_op jit(solution)/shard_map/ppermute | solution.py:40
  (12 other events, 76.0 us)
where the time goes:
time: 148 us; the launch traced here: 147 us
  other arithmetic  55.4 us (37%)
  starting transfers between devices  54.2 us (37%)
  local copies, waits for them, and re-layouts  17 us (11%)
  matrix products  15.2 us (10%)
  waiting for transfers between devices  3.49 us (2%)
  between operations  1.99 us (1%)
    ppermute x8, starting transfers between devices, padded(): lax.ppermute(lax.slice_in_dim(block, 0, width, axis=dim), axis, backward)  29.2 us
    reduce_sum x4, other arithmetic, one_group(): summed = summed + jnp.sum(offset * closeness[None, :, :], axis=2)  26 us
    ppermute x8, starting transfers between devices, padded(): lax.ppermute(lax.slice_in_dim(block, block.shape[dim] - width, None, axis...  25 us
    dot_general x9, matrix products, window_cube(): jnp.einsum('vtn,tl->vnl', scattered_loads, along_depth, preferred_element...  12.7 us
    mul x12, other arithmetic, one_group(): jnp.exp(-jnp.sum(offset * offset, axis=0) / (2.0 * PAIR_WIDTH * PAIR_WIDTH))  7.98 us
    reduce_sum x7, other arithmetic, gaussian_rows(): return bumps / jnp.sum(bumps, axis=1, keepdims=True)  6.11 us
    reduce_sum x2, other arithmetic, one_group(): jnp.sum(offset * offset, axis=0)  3.62 us
    ppermute x8, waiting for transfers between devices, padded(): lax.ppermute(lax.slice_in_dim(block, 0, width, axis=dim), axis, backward)  3.46 us
  transfers between devices with their start and end apart: 16, of which 3 were waited for; matrix products, arithmetic and copies ran while one was open for 21% of the time, Pallas kernels for 0%

commit v1 on v0

v1 whole, which is shorter than its diff:
```python
import functools
import math

import jax
import jax.numpy as jnp
import numpy as np
from jax import lax
from jax.experimental import pallas as pl
from jax.experimental.pallas import tpu as pltpu
from jax.sharding import PartitionSpec as P

P_DEV = 1024
E_DEV = 32
BINS_THIRD_AXIS = 512
BX = 16
BY = 16
MARGIN = 4
QUANT = 64
CAP = 64

GLL_NODES = (
    -1.0,
    -0.8717401485096066,
    -0.5917001814331423,
    -0.2092992179024789,
    0.2092992179024789,
    0.5917001814331423,
    0.8717401485096066,
    1.0,
)
STIFFNESS = 0.5
PAIR_WIDTH = 0.3
FILTER_BINS = 3.0

f32 = jnp.float32
bf16 = jnp.bfloat16
MESH = pl.DeviceIdType.MESH

LOG2E = math.log2(math.e)
HEIGHT = BINS_THIRD_AXIS / BX
PAIR_SCALE = math.sqrt(LOG2E) / PAIR_WIDTH
DEPTH_SCALE = math.sqrt(LOG2E / 2.0) / (FILTER_BINS / BX)
EDGE_RATE = LOG2E / (2.0 * (FILTER_BINS / BX) ** 2)
FIELD_SCALE = BX * BY * BINS_THIRD_AXIS / P_DEV

STEPS = tuple((k // 3 - 1, k % 3 - 1) for k in range(9) if k != 4)
OWN = 8
ROWS_Q = 64


def basis_pieces():
    points = -1.0 + (2.0 * np.arange(QUANT) + 1.0) / QUANT
    lagrange = np.ones((QUANT, 8))
    for node_a in range(8):
        for node_b in range(8):
            if node_b != node_a:
                lagrange[:, node_a] *= (points - GLL_NODES[node_b]) / (
                    GLL_NODES[node_a] - GLL_NODES[node_b]
                )
    rest = lagrange.astype(np.float32).T
    pieces = []
    for _ in range(3):
        piece = rest.astype(bf16)
        pieces.append(piece)
        rest = rest - piece.astype(np.float32)
    pieces.append(np.zeros_like(pieces[0]))
    return np.concatenate(pieces, axis=0)


def rows_iota(shape):
    return lax.broadcasted_iota(jnp.int32, shape, 0)


def split3(x):
    high = x.astype(bf16).astype(f32)
    rest = x - high
    middle = rest.astype(bf16).astype(f32)
    low = (rest - middle).astype(bf16).astype(f32)
    return high, middle, low


def kernel(
    grid_x, grid_y,
    frac_ref, vel_ref, drag_ref, vol_ref, owner_ref, element_ref, coords_ref, table_ref, basis_ref,
    force_ref, field_ref,
    pos_send, pos_recv, req_send, req_recv, val_send, val_recv, load_send, load_recv,
    xs, fq_t, cols, feat, fp, g_ref, weights, own_val, pair_acc, wz, spread_c, spread_e, wx_ref, wy_ref,
    wx4, wy4,
    pos_ss, pos_rs, req_ss, req_rs, val_ss, val_rs, load_ss, load_rs,
):
    me_x = lax.axis_index("gx")
    me_y = lax.axis_index("gy")
    ids = []
    present = []
    for dx, dy in STEPS:
        tx, ty = me_x + dx, me_y + dy
        ids.append((lax.rem(tx + grid_x, grid_x), lax.rem(ty + grid_y, grid_y)))
        inside = (tx >= 0) & (tx < grid_x) & (ty >= 0) & (ty < grid_y)
        present.append(jnp.where(inside, 1.0, 0.0).astype(f32))

    barrier = pltpu.get_barrier_semaphore()
    for n in range(8):
        pl.semaphore_signal(barrier, inc=1, device_id=ids[n], device_id_type=MESH)

    def remote(src, dst, ss, rs, n):
        return pltpu.make_async_remote_copy(
            src_ref=src, dst_ref=dst.at[7 - n], send_sem=ss.at[n], recv_sem=rs.at[7 - n],
            device_id=ids[n], device_id_type=MESH,
        )

    pos_copies = [remote(pos_send, pos_recv, pos_ss, pos_rs, n) for n in range(8)]
    req_copies = [remote(req_send.at[n // 2], req_recv, req_ss, req_rs, n) for n in range(8)]
    val_copies = [remote(val_send.at[n // 2], val_recv, val_ss, val_rs, n) for n in range(8)]
    load_copies = [remote(load_send, load_recv, load_ss, load_rs, n) for n in range(8)]

    fz = frac_ref[2:3, :]
    z_own = fz * HEIGHT * DEPTH_SCALE

    def sum_step(i, acc):
        at = (rows_iota((64, P_DEV)) + i * 64).astype(f32)
        d = z_own - (at + 0.5) * (DEPTH_SCALE / BX)
        bumps = jnp.exp2(-(d * d))
        return acc + jnp.sum(bumps.reshape(8, 8, P_DEV), axis=0)

    partial = lax.fori_loop(0, BINS_THIRD_AXIS // 64, sum_step, jnp.zeros((8, P_DEV), f32))
    total = jnp.sum(partial, axis=0, keepdims=True)
    pos_send[0:3, :] = frac_ref[...]
    pos_send[3:4, :] = -LOG2E * jnp.log(total)

    pl.semaphore_wait(barrier, 8)
    for copy in pos_copies:
        copy.start()

    row8 = rows_iota((8, 1))
    offsets = jnp.zeros((8, 1), jnp.int32)
    for n, (dx, dy) in enumerate(STEPS):
        offsets = jnp.where(row8 == n, dx * grid_y + dy, offsets)
    delta = owner_ref[...] - (me_x * grid_y + me_y)
    chosen = jnp.where(delta == offsets, 1.0, 0.0).astype(f32)
    blocks = [chosen[:, 128 * b : 128 * b + 128] for b in range(8)]
    stacked = jnp.concatenate(blocks, axis=0).astype(bf16)
    lower = rows_iota((128, 128)) < lax.broadcasted_iota(jnp.int32, (128, 128), 1)
    earlier = jnp.dot(stacked, jnp.where(lower, 1.0, 0.0).astype(bf16), preferred_element_type=f32)
    base = (row8 * CAP).astype(f32)
    ranked = []
    for b in range(8):
        ranked.append(earlier[8 * b : 8 * b + 8] + base)
        base = base + jnp.sum(blocks[b], axis=1, keepdims=True)
    ranked = jnp.concatenate(ranked, axis=1)
    is_remote = jnp.sum(chosen, axis=0, keepdims=True)
    place = jnp.sum(chosen * ranked, axis=0, keepdims=True)
    slot = jnp.where(is_remote > 0.0, place, -1.0)
    for i in range(8):
        at = (rows_iota((64, 1)) + i * 64).astype(f32)
        g_ref[64 * i : 64 * i + 64, :] = jnp.where(slot == at, 1.0, 0.0).astype(bf16)

    xs[0:1, :] = element_ref[...].astype(f32)
    xs[1:4, :] = coords_ref[...].astype(f32)
    xs[4:8, :] = jnp.zeros((4, P_DEV), f32)
    payload = xs[...]
    payload16 = jnp.concatenate([payload, jnp.zeros((8, P_DEV), f32)], axis=0).astype(bf16)
    outgoing = lax.dot_general(
        payload16, g_ref[...], (((1,), (1,)), ((), ())), preferred_element_type=f32
    )
    for j in range(4):
        req_send[j] = outgoing[0:8, 128 * j : 128 * j + 128]
    for copy in req_copies:
        copy.start()

    def interpolate(requests):
        slots = requests.shape[1]
        levels = rows_iota((QUANT, 1)).astype(f32)
        factors = []
        for axis in range(3):
            select = jnp.where(requests[1 + axis : 2 + axis, :] == levels, 1.0, 0.0).astype(bf16)
            pieces = jnp.dot(basis_ref[...], select, preferred_element_type=f32)
            factors.append(pieces[0:8] + pieces[8:16] + pieces[16:24])
        for a in range(8):
            plane = factors[0][a : a + 1, :] * factors[1]
            for b in range(0, 8, 2):
                pair = jnp.concatenate(
                    [plane[b : b + 1, :] * factors[2], plane[b + 1 : b + 2, :] * factors[2]], axis=0
                )
                at = 64 * a + 8 * b
                weights[at : at + 16, :] = pair.astype(bf16)
        projected = jnp.dot(table_ref[...], weights[...], preferred_element_type=f32)
        element = requests[0:1, :]
        values = jnp.zeros((8, slots), f32)
        for e in range(E_DEV):
            values = values + jnp.where(element == float(e), projected[8 * e : 8 * e + 8, :], 0.0)
        return values.astype(bf16).astype(f32)

    def place_rows(dx, dy):
        row = rows_iota((8, 1))
        factor = jnp.where(row == 2, HEIGHT * PAIR_SCALE, PAIR_SCALE)
        shift = jnp.where(row == 0, dx * PAIR_SCALE, jnp.where(row == 1, dy * PAIR_SCALE, -0.5 * HEIGHT * PAIR_SCALE))
        return jnp.where(row < 3, xs[...] * factor + shift, 0.0)

    def features(m, dx, dy, weight):
        row = rows_iota((8, 1))
        where_at = place_rows(dx, dy)
        half = 0.5 * jnp.sum(where_at * where_at, axis=0, keepdims=True)
        vector = jnp.where(row == 3, -half, jnp.where(row == 4, 1.0, where_at))
        q1, q2, q3 = split3(vector)
        raw = xs[...]
        stack = jnp.concatenate([q1, q2, q1, q2, q3, q1, raw, jnp.zeros_like(raw)], axis=0)
        turned = stack.T
        fq_t[m] = turned.astype(bf16)
        cols[m] = turned[:, 48:56]
        if weight is not None:
            q1, q2, q3 = q1 * weight, q2 * weight, q3 * weight
        feat[m] = jnp.concatenate([q1, q2, q3, jnp.zeros_like(q1)], axis=0).astype(bf16)
        return where_at

    xs[0:4, :] = pos_send[...]
    xs[4:8, :] = jnp.zeros((4, P_DEV), f32)
    own_at = features(OWN, 0, 0, None)
    row8 = rows_iota((8, 1))
    half_own = 0.5 * jnp.sum(own_at * own_at, axis=0, keepdims=True)
    p1, p2, p3 = split3(jnp.where(row8 == 3, 1.0, jnp.where(row8 == 4, -half_own, own_at)))
    blank = jnp.zeros_like(p1)
    fp[...] = jnp.concatenate([p1, p1, p2, p2, p1, p3, blank, blank], axis=0).astype(bf16)

    def pair_block(m):
        exponent = jnp.dot(fq_t[m], fp[...], preferred_element_type=f32)
        closeness = jnp.exp2(exponent).astype(bf16)
        return jnp.dot(feat[m], closeness, preferred_element_type=f32)

    pair_acc[...] = pair_block(OWN)
    for half in range(2):
        own_val[:, 512 * half : 512 * half + 512] = interpolate(payload[:, 512 * half : 512 * half + 512])

    for copy in pos_copies:
        copy.wait_recv()
    for m, (dx, dy) in enumerate(STEPS):
        xs[0:4, :] = pos_recv[m]
        features(m, dx, dy, present[m])

    for copy in req_copies:
        copy.wait_recv()
    low_half = lax.broadcasted_iota(jnp.int32, (8, 128), 1) < CAP
    arrived = jnp.concatenate(
        [jnp.where(low_half, req_recv[2 * j + 1], req_recv[2 * j]) for j in range(4)], axis=1
    )
    served = interpolate(arrived)
    for j in range(4):
        val_send[j] = served[:, 128 * j : 128 * j + 128]
    for copy in val_copies:
        copy.start()

    def pair_step(m, carry):
        pair_acc[...] += pair_block(m)
        return carry

    lax.fori_loop(0, 8, pair_step, 0)

    for copy in val_copies:
        copy.wait_recv()
    returned = jnp.concatenate(
        [jnp.where(low_half, val_recv[2 * j], val_recv[2 * j + 1]) for j in range(4)], axis=1
    )
    returned16 = jnp.concatenate([returned, jnp.zeros((8, 512), f32)], axis=0).astype(bf16)
    fetched = jnp.dot(returned16, g_ref[...], preferred_element_type=f32)[0:8]
    fetched = jnp.where(is_remote > 0.0, fetched, own_val[...])
    gradient = pltpu.roll(fetched, 4, axis=0)
    sums = pair_acc[...]
    sums = sums[0:8] + sums[8:16] + sums[16:24]
    pair = (STIFFNESS / PAIR_SCALE) * (own_at * sums[4:5, :] - sums)
    xs[0:3, :] = vel_ref[...]
    volume = vol_ref[...]
    force = drag_ref[...] * (fetched - xs[...]) - volume * gradient + pair
    force_ref[...] = force[0:3]
    loads = jnp.where(row8 == 3, volume, force)
    load_send[...] = loads[0:4]
    for copy in load_copies:
        copy.start()

    def edge_rows(fraction, rows):
        d = fraction - (rows.astype(f32) + (0.5 - MARGIN)) * (1.0 / BX)
        return jnp.exp2((d * d) * (-EDGE_RATE))

    row24 = rows_iota((24, 1))
    order_y = jnp.where(row24 < 16, row24 + 4, jnp.where(row24 < 20, row24 - 16, row24))

    def all_edges(fx, fy):
        bump_x = edge_rows(fx, row24)
        bump_y = edge_rows(fy, order_y)
        scale_x = 1.0 / jnp.sum(bump_x, axis=0, keepdims=True)
        scale_y = 1.0 / jnp.sum(bump_y, axis=0, keepdims=True)
        wx_ref[...] = bump_x * scale_x
        wy_ref[...] = bump_y * scale_y

    at_z = (lax.broadcasted_iota(jnp.int32, (1, BINS_THIRD_AXIS), 1).astype(f32) + 0.5) * (DEPTH_SCALE / BX)

    def depth_rows(m):
        def depth_step(i, carry):
            r0 = pl.multiple_of(i * 64, 64)
            block = cols[m, pl.ds(r0, 64), :]
            d = block[:, 2:3] * (HEIGHT * DEPTH_SCALE) - at_z
            wz[m, pl.ds(r0, 64), :] = jnp.exp2(block[:, 3:4] - d * d).astype(bf16)
            return carry

        lax.fori_loop(0, P_DEV // 64, depth_step, 0)

    depth_rows(OWN)
    all_edges(pos_send[0:1, :], pos_send[1:2, :])

    def spread_step(a, carry):
        plane = wx_ref[pl.ds(a + MARGIN, 1), :] * wy_ref[0:16, :]
        for c in range(4):
            r0 = pl.multiple_of((c * 16 + a) * 16, 16)
            spread_c[pl.ds(r0, 16), :] = (plane * (load_send[c : c + 1, :] * FIELD_SCALE)).astype(bf16)
        return carry

    lax.fori_loop(0, 16, spread_step, 0)

    for c in range(4):
        part = jnp.dot(spread_c[256 * c : 256 * c + 256, :], wz[OWN], preferred_element_type=f32)
        field_ref[c] = part.reshape(16, 16, BINS_THIRD_AXIS)

    def neighbour_depth(m, carry):
        depth_rows(m)
        return carry

    lax.fori_loop(0, 8, neighbour_depth, 0)

    for copy in load_copies:
        copy.wait_recv()
    for m, (dx, dy) in enumerate(STEPS):
        all_edges(pos_recv[m, 0:1, :], pos_recv[m, 1:2, :])
        loads_m = [load_recv[m, c : c + 1, :] * (FIELD_SCALE * present[m]) for c in range(4)]
        source_x = {-1: 20, 0: 4, 1: 0}[dx]
        target_x = {-1: 0, 0: 0, 1: 12}[dx]
        count_x = 16 if dx == 0 else 4
        if dy == 0:
            for a in range(count_x):
                plane = wx_ref[source_x + a : source_x + a + 1, :] * wy_ref[0:16, :]
                for c in range(4):
                    r0 = (c * count_x + a) * 16
                    spread_e[r0 : r0 + 16, :] = (plane * loads_m[c]).astype(bf16)
            part = jnp.dot(spread_e[...], wz[m], preferred_element_type=f32)
            for c in range(4):
                field_ref[c, target_x : target_x + 4] += part[64 * c : 64 * c + 64].reshape(4, 16, BINS_THIRD_AXIS)
        else:
            first = 20 if dy == -1 else 16
            target_y = 0 if dy == -1 else 12
            wy4[0:4, :] = wy_ref[first : first + 4, :]
            wy4[4:8, :] = wy_ref[first : first + 4, :]
            top = rows_iota((8, 1)) < 4
            for a in range(0, count_x, 4):
                planes = []
                for pair_at in (a, a + 2):
                    s = source_x + pair_at
                    planes.append(jnp.where(top, wx_ref[s : s + 1, :], wx_ref[s + 1 : s + 2, :]) * wy4[...])
                plane = jnp.concatenate(planes, axis=0)
                for c in range(4):
                    r0 = (c * count_x + a) * 4
                    spread_e[r0 : r0 + 16, :] = (plane * loads_m[c]).astype(bf16)
            used = 16 * count_x
            part = jnp.dot(spread_e[0:used, :], wz[m], preferred_element_type=f32)
            for c in range(4):
                for a in range(count_x):
                    r0 = (c * count_x + a) * 4
                    field_ref[c, target_x + a, target_y : target_y + 4, :] += part[r0 : r0 + 4, :]

    for copy in pos_copies + req_copies + val_copies + load_copies:
        copy.wait_send()


def body(fractions, velocity, drag_rate, volume, owner, element, coords, fluid):
    grid_x = lax.axis_size("gx")
    grid_y = lax.axis_size("gy")
    nodes = fluid.reshape(E_DEV, 6, 512)
    nothing = jnp.zeros((E_DEV, 1, 512), bf16)
    table = jnp.concatenate([nodes[:, 0:3], nothing, nodes[:, 3:6], nothing], axis=1).reshape(256, 512)
    vmem = pl.BlockSpec(memory_space=pltpu.VMEM)
    dma = pltpu.SemaphoreType.DMA((8,))
    force, field = pl.pallas_call(
        functools.partial(kernel, grid_x, grid_y),
        out_shape=(
            jax.ShapeDtypeStruct((3, P_DEV), f32),
            jax.ShapeDtypeStruct((4, BX, BY, BINS_THIRD_AXIS), f32),
        ),
        in_specs=[vmem] * 9,
        out_specs=(vmem, vmem),
        scratch_shapes=[
            pltpu.VMEM((4, P_DEV), f32),
            pltpu.VMEM((8, 4, P_DEV), f32),
            pltpu.VMEM((4, 8, 128), f32),
            pltpu.VMEM((8, 8, 128), f32),
            pltpu.VMEM((4, 8, 128), f32),
            pltpu.VMEM((8, 8, 128), f32),
            pltpu.VMEM((4, P_DEV), f32),
            pltpu.VMEM((8, 4, P_DEV), f32),
            pltpu.VMEM((8, P_DEV), f32),
            pltpu.VMEM((9, P_DEV, ROWS_Q), bf16),
            pltpu.VMEM((9, P_DEV, 8), f32),
            pltpu.VMEM((9, 32, P_DEV), bf16),
            pltpu.VMEM((ROWS_Q, P_DEV), bf16),
            pltpu.VMEM((8 * CAP, P_DEV), bf16),
            pltpu.VMEM((512, 512), bf16),
            pltpu.VMEM((8, P_DEV), f32),
            pltpu.VMEM((32, P_DEV), f32),
            pltpu.VMEM((9, P_DEV, BINS_THIRD_AXIS), bf16),
            pltpu.VMEM((1024, P_DEV), bf16),
            pltpu.VMEM((256, P_DEV), bf16),
            pltpu.VMEM((24, P_DEV), f32),
            pltpu.VMEM((24, P_DEV), f32),
            pltpu.VMEM((24, P_DEV), f32),
            pltpu.VMEM((8, P_DEV), f32),
        ]
        + [dma] * 8,
        compiler_params=pltpu.CompilerParams(
            collective_id=0, has_side_effects=True, vmem_limit_bytes=50 * 1024 * 1024
        ),
        name="particle_step",
    )(
        fractions.reshape(3, P_DEV),
        velocity.reshape(3, P_DEV),
        drag_rate.reshape(1, P_DEV),
        volume.reshape(1, P_DEV),
        owner.reshape(1, P_DEV),
        element.reshape(1, P_DEV),
        coords.reshape(3, P_DEV),
        table,
        jnp.asarray(basis_pieces()),
    )
    return force.reshape(1, 1, 3, P_DEV), field


def solution(mesh):
    return jax.shard_map(
        body,
        mesh=mesh,
        in_specs=(
            P("gx", "gy", None, None),
            P("gx", "gy", None, None),
            P("gx", "gy", None),
            P("gx", "gy", None),
            P("gx", "gy", None, None),
            P("gx", "gy", None),
            P("gx", "gy", None, None),
            P("gx", "gy", None, None, None),
        ),
        out_specs=(P("gx", "gy", None, None), P(None, "gx", "gy", None)),
        check_vma=False,
    )
```

time: 148 us -> 52.1 us (0.35)
  the two profiles are of different devices: /device:TPU:7 before, /device:TPU:1 now
where the time goes in v1:
time: 52.1 us; the launch traced here: 51.6 us
  Pallas kernels  43 us (83%)
  local copies, waits for them, and re-layouts  7.93 us (15%)
  between operations  0.68 us (1%)
    pallas_call x1, Pallas kernels, body(): pl.pallas_call(functools.partial(kernel, grid_x, grid_y), out_shape=(jax....  43 us
    unnamed x14, local copies, waits for them, and re-layouts  6.81 us

profile of v1, /device:TPU:1, one launch (start us, length us, event | category | flops | bytes accessed | tf_op | source)
XLA Modules:
  0.0 51.6 jit_solution(4809172371912558161)
XLA Ops:
  0.6 0.7 %copy.21 = s32[1,1,3,1024]{3,2,1,0:T(4,128)S(1)} copy(s32[1,1,3,1024]{3,1,2,0:T(1,128)} %param.15) | data formatting | bytes 24576
  1.3 0.7 %copy_bitcast_fusion.2 = (f32[3,1024]{1,0:T(4,128)S(1)}, f32[3,1024]{1,0:T(4,128)S(1)}) fusion(f32[1,1,3,1024]{3,1,2,0:T(1,128)} %param.10, f32[1,1,3,1024]{3,1,2,0:T(1,128)} %param.9), kind=kLoop, calls=%fused_computation.3 | loop fusion | bytes 49152
  2.1 1.0 %fusion = (bf16[32,3,512]{2,0,1:T(8,128)(2,1)S(1)}, bf16[32,3,512]{2,0,1:T(8,128)(2,1)S(1)}) fusion(bf16[32,6,512]{2,0,1:T(8,128)(2,1)} %bitcast.23), kind=kLoop, calls=%fused_computation.5 | loop fusion | bytes 393216 | tf_op jit(solution)/shard_map/slice | solution.py:375
  3.1 0.2 copy.20
  3.3 0.0 copy-start
  3.3 0.7 %copy-done = bf16[32,64]{1,0:T(8,128)(2,1)S(1)} copy-done((bf16[32,64]{1,0:T(8,128)(2,1)S(1)}, bf16[32,64]{1,0:T(8,128)(2,1)}, u32[]{:S(2)}) %copy-start) | copy-done | bytes 4120
  4.0 0.0 copy-start.1
  4.0 0.7 %copy-done.1 = f32[1,1,1024]{2,1,0:T(1,128)S(1)} copy-done((f32[1,1,1024]{2,1,0:T(1,128)S(1)}, f32[1,1,1024]{2,1,0:T(1,128)}, u32[]{:S(2)}) %copy-start.1) | copy-done | bytes 4120
  4.6 0.0 copy-start.2
  4.6 0.7 %copy-done.2 = f32[1,1,1024]{2,1,0:T(1,128)S(1)} copy-done((f32[1,1,1024]{2,1,0:T(1,128)S(1)}, f32[1,1,1024]{2,1,0:T(1,128)}, u32[]{:S(2)}) %copy-start.2) | copy-done | bytes 4120
  5.3 0.0 copy-start.3
  5.3 0.7 %copy-done.3 = s32[1,1,1024,1]{2,3,1,0:T(1,128)S(1)} copy-done((s32[1,1,1024,1]{2,3,1,0:T(1,128)S(1)}, s32[1,1,1024,1]{2,3,1,0:T(1,128)}, u32[]{:S(2)}) %copy-start.3) | copy-done | bytes 4120
  6.0 0.0 copy-start.4
  6.0 0.7 %copy-done.4 = s32[1,1,1024]{2,1,0:T(1,128)S(1)} copy-done((s32[1,1,1024]{2,1,0:T(1,128)S(1)}, s32[1,1,1024]{2,1,0:T(1,128)}, u32[]{:S(2)}) %copy-start.4) | copy-done | bytes 4120
  6.7 43.0 %particle_step.1 = (f32[3,1024]{1,0:T(4,128)S(1)}, f32[4,16,16,512]{3,2,1,0:T(8,128)S(1)}) custom-call(f32[3,1024]{1,0:T(4,128)S(1)} %get-tuple-element.11.frac_ref, f32[3,1024]{1,0:T(4,128)S(1)} %get-tuple-element.10.vel_ref, f32[1,1024]{1,0:T(1,128)S(1)} %bitcast.19, f32[1,1024]{1,0:T(1,128)S(1)} %bitcast.20, s32[1,1024]{1,0:T(1,128)S(1)} %bitcast.21, ...), custom_call_target="tpu_custom_call" | custom-call | tf_op jit(solution)/shard_map/particle_step/pallas_call | solution.py:378
  49.7 0.6 %copy.12 = f32[1,1,3,1024]{3,1,2,0:T(1,128)} copy(f32[1,1,3,1024]{3,2,1,0:T(4,128)S(1)} %bitcast.18) | data formatting | bytes 24576
  50.3 1.3 %copy.23 = f32[4,16,16,512]{3,2,1,0:T(8,128)} copy(f32[4,16,16,512]{3,2,1,0:T(8,128)S(1)} %get-tuple-element.15) | data formatting | bytes 4194304
  (2 shorter events, 0.0 us)
Async XLA Ops:
  3.3 0.7 %copy-start = (bf16[32,64]{1,0:T(8,128)(2,1)S(1)}, bf16[32,64]{1,0:T(8,128)(2,1)}, u32[]{:S(2)}) copy-start(bf16[32,64]{1,0:T(8,128)(2,1)} %constant.4.clone.basis_ref) | copy-start | bytes 12292
  4.0 0.7 %copy-start.1 = (f32[1,1,1024]{2,1,0:T(1,128)S(1)}, f32[1,1,1024]{2,1,0:T(1,128)}, u32[]{:S(2)}) copy-start(f32[1,1,1024]{2,1,0:T(1,128)} %param.11) | copy-start | bytes 12292
  4.6 0.7 %copy-start.2 = (f32[1,1,1024]{2,1,0:T(1,128)S(1)}, f32[1,1,1024]{2,1,0:T(1,128)}, u32[]{:S(2)}) copy-start(f32[1,1,1024]{2,1,0:T(1,128)} %param.12) | copy-start | bytes 12292
  5.3 0.7 %copy-start.3 = (s32[1,1,1024,1]{2,3,1,0:T(1,128)S(1)}, s32[1,1,1024,1]{2,3,1,0:T(1,128)}, u32[]{:S(2)}) copy-start(s32[1,1,1024,1]{2,3,1,0:T(1,128)} %param.13) | copy-start | bytes 12292
  6.0 0.7 %copy-start.4 = (s32[1,1,1024]{2,1,0:T(1,128)S(1)}, s32[1,1,1024]{2,1,0:T(1,128)}, u32[]{:S(2)}) copy-start(s32[1,1,1024]{2,1,0:T(1,128)} %param.14) | copy-start | bytes 12292

commit v2 on v1

--- a/solution.py
+++ b/solution.py
@@ -67,6 +67,22 @@
     return np.concatenate(pieces, axis=0)
 
 
+def depth_pieces():
+    centres = ((np.arange(BINS_THIRD_AXIS) + 0.5) / BX - 0.5 * HEIGHT) * DEPTH_SCALE
+    rows = np.zeros((8, BINS_THIRD_AXIS))
+    rows[2] = 2.0 * centres * (DEPTH_SCALE / PAIR_SCALE)
+    rows[4] = -centres * centres
+    pieces = []
+    for _ in range(3):
+        piece = rows.astype(bf16)
+        pieces.append(piece)
+        rows = rows - piece.astype(np.float64)
+    first, second, third = pieces
+    last = np.zeros((16, BINS_THIRD_AXIS))
+    last[0:3] = 1.0
+    return np.concatenate([first, first, second, second, first, third, last.astype(bf16)], axis=0)
+
+
 def rows_iota(shape):
     return lax.broadcasted_iota(jnp.int32, shape, 0)
 
@@ -81,13 +97,24 @@
 
 def kernel(
     grid_x, grid_y,
-    frac_ref, vel_ref, drag_ref, vol_ref, owner_ref, element_ref, coords_ref, table_ref, basis_ref,
+    frac_in, vel_in, drag_in, vol_in, owner_in, element_in, coords_in, table_in, basis_in, depth_in,
+    force_out, field_out,
     force_ref, field_ref,
+    frac_ref, vel_ref, drag_ref, vol_ref, owner_ref, element_ref, coords_ref, table_ref, basis_ref, depth_ref,
     pos_send, pos_recv, req_send, req_recv, val_send, val_recv, load_send, load_recv,
-    xs, fq_t, cols, feat, fp, g_ref, weights, own_val, pair_acc, wz, spread_c, spread_e, wx_ref, wy_ref,
+    xs, fq_t, feat, fp, g_ref, weights, own_val, pair_acc, wz, spread_c, spread_e, wx_ref, wy_ref,
     wx4, wy4,
-    pos_ss, pos_rs, req_ss, req_rs, val_ss, val_rs, load_ss, load_rs,
+    in_ss, out_ss, pos_ss, pos_rs, req_ss, req_rs, val_ss, val_rs, load_ss, load_rs,
 ):
+    inputs = (
+        (frac_in, frac_ref), (owner_in, owner_ref), (element_in, element_ref), (coords_in, coords_ref),
+        (basis_in, basis_ref), (table_in, table_ref), (vel_in, vel_ref), (drag_in, drag_ref), (vol_in, vol_ref),
+        (depth_in, depth_ref),
+    )
+    loads_in = [pltpu.make_async_copy(src, dst, in_ss.at[k]) for k, (src, dst) in enumerate(inputs)]
+    for copy in loads_in:
+        copy.start()
+
     me_x = lax.axis_index("gx")
     me_y = lax.axis_index("gy")
     ids = []
@@ -113,7 +140,8 @@
     val_copies = [remote(val_send.at[n // 2], val_recv, val_ss, val_rs, n) for n in range(8)]
     load_copies = [remote(load_send, load_recv, load_ss, load_rs, n) for n in range(8)]
 
-    fz = frac_ref[2:3, :]
+    loads_in[0].wait()
+    fz = frac_ref[2]
     z_own = fz * HEIGHT * DEPTH_SCALE
 
     def sum_step(i, acc):
@@ -124,13 +152,16 @@
 
     partial = lax.fori_loop(0, BINS_THIRD_AXIS // 64, sum_step, jnp.zeros((8, P_DEV), f32))
     total = jnp.sum(partial, axis=0, keepdims=True)
-    pos_send[0:3, :] = frac_ref[...]
+    for d in range(3):
+        pos_send[d : d + 1, :] = frac_ref[d]
     pos_send[3:4, :] = -LOG2E * jnp.log(total)
 
     pl.semaphore_wait(barrier, 8)
     for copy in pos_copies:
         copy.start()
 
+    for copy in loads_in[1:]:
+        copy.wait()
     row8 = rows_iota((8, 1))
     offsets = jnp.zeros((8, 1), jnp.int32)
     for n, (dx, dy) in enumerate(STEPS):
@@ -155,7 +186,8 @@
         g_ref[64 * i : 64 * i + 64, :] = jnp.where(slot == at, 1.0, 0.0).astype(bf16)
 
     xs[0:1, :] = element_ref[...].astype(f32)
-    xs[1:4, :] = coords_ref[...].astype(f32)
+    for d in range(3):
+        xs[1 + d : 2 + d, :] = coords_ref[d].astype(f32)
     xs[4:8, :] = jnp.zeros((4, P_DEV), f32)
     payload = xs[...]
     payload16 = jnp.concatenate([payload, jnp.zeros((8, P_DEV), f32)], axis=0).astype(bf16)
@@ -184,10 +216,12 @@
                 at = 64 * a + 8 * b
                 weights[at : at + 16, :] = pair.astype(bf16)
         projected = jnp.dot(table_ref[...], weights[...], preferred_element_type=f32)
-        element = requests[0:1, :]
-        values = jnp.zeros((8, slots), f32)
-        for e in range(E_DEV):
-            values = values + jnp.where(element == float(e), projected[8 * e : 8 * e + 8, :], 0.0)
+        mine = requests[0:1, :] == rows_iota((E_DEV, 1)).astype(f32)
+        values = [
+            jnp.sum(jnp.where(mine, projected[E_DEV * k : E_DEV * k + E_DEV, :], 0.0), axis=0, keepdims=True)
+            for k in range(6)
+        ]
+        values = jnp.concatenate(values + [jnp.zeros((2, slots), f32)], axis=0)
         return values.astype(bf16).astype(f32)
 
     def place_rows(dx, dy):
@@ -202,11 +236,11 @@
         half = 0.5 * jnp.sum(where_at * where_at, axis=0, keepdims=True)
         vector = jnp.where(row == 3, -half, jnp.where(row == 4, 1.0, where_at))
         q1, q2, q3 = split3(vector)
-        raw = xs[...]
-        stack = jnp.concatenate([q1, q2, q1, q2, q3, q1, raw, jnp.zeros_like(raw)], axis=0)
-        turned = stack.T
-        fq_t[m] = turned.astype(bf16)
-        cols[m] = turned[:, 48:56]
+        depth = where_at[2:3, :] * (DEPTH_SCALE / PAIR_SCALE)
+        h1, h2, h3 = split3(xs[3:4, :] - depth * depth)
+        level = jnp.where(row == 0, h1, jnp.where(row == 1, h2, jnp.where(row == 2, h3, 0.0)))
+        stack = jnp.concatenate([q1, q2, q1, q2, q3, q1, level, jnp.zeros_like(level)], axis=0)
+        fq_t[m] = stack.T.astype(bf16)
         if weight is not None:
             q1, q2, q3 = q1 * weight, q2 * weight, q3 * weight
         feat[m] = jnp.concatenate([q1, q2, q3, jnp.zeros_like(q1)], axis=0).astype(bf16)
@@ -226,15 +260,47 @@
         closeness = jnp.exp2(exponent).astype(bf16)
         return jnp.dot(feat[m], closeness, preferred_element_type=f32)
 
+    def edge_rows(fraction, rows):
+        d = fraction - (rows.astype(f32) + (0.5 - MARGIN)) * (1.0 / BX)
+        return jnp.exp2((d * d) * (-EDGE_RATE))
+
+    row24 = rows_iota((24, 1))
+    order_y = jnp.where(row24 < 16, row24 + 4, jnp.where(row24 < 20, row24 - 16, row24))
+
+    def all_edges(fx, fy):
+        bump_x = edge_rows(fx, row24)
+        bump_y = edge_rows(fy, order_y)
+        scale_x = 1.0 / jnp.sum(bump_x, axis=0, keepdims=True)
+        scale_y = 1.0 / jnp.sum(bump_y, axis=0, keepdims=True)
+        wx_ref[...] = bump_x * scale_x
+        wy_ref[...] = bump_y * scale_y
+
+    def depth_rows(m):
+        exponent = jnp.dot(fq_t[m], depth_ref[...], preferred_element_type=f32)
+        wz[m] = jnp.exp2(exponent).astype(bf16)
+
     pair_acc[...] = pair_block(OWN)
     for half in range(2):
         own_val[:, 512 * half : 512 * half + 512] = interpolate(payload[:, 512 * half : 512 * half + 512])
-
-    for copy in pos_copies:
-        copy.wait_recv()
-    for m, (dx, dy) in enumerate(STEPS):
+    all_edges(pos_send[0:1, :], pos_send[1:2, :])
+    depth_rows(OWN)
+
+    def arrive(m):
+        pos_copies[7 - m].wait_recv()
+
+    def neighbour_features(m):
         xs[0:4, :] = pos_recv[m]
-        features(m, dx, dy, present[m])
+        features(m, STEPS[m][0], STEPS[m][1], present[m])
+
+    for m in (3, 4):
+        arrive(m)
+    for m in (3, 4):
+        neighbour_features(m)
+    pair_acc[...] += pair_block(3) + pair_block(4)
+    for m in (0, 1, 2, 5, 6, 7):
+        arrive(m)
+    for m in (0, 1, 2, 5, 6, 7):
+        neighbour_features(m)
 
     for copy in req_copies:
         copy.wait_recv()
@@ -249,10 +315,10 @@
         copy.start()
 
     def pair_step(m, carry):
-        pair_acc[...] += pair_block(m)
+        pair_acc[...] += pair_block(m) + pair_block(m + 5)
         return carry
 
-    lax.fori_loop(0, 8, pair_step, 0)
+    lax.fori_loop(0, 3, pair_step, 0)
 
     for copy in val_copies:
         copy.wait_recv()
@@ -262,48 +328,22 @@
     returned16 = jnp.concatenate([returned, jnp.zeros((8, 512), f32)], axis=0).astype(bf16)
     fetched = jnp.dot(returned16, g_ref[...], preferred_element_type=f32)[0:8]
     fetched = jnp.where(is_remote > 0.0, fetched, own_val[...])
-    gradient = pltpu.roll(fetched, 4, axis=0)
+    gradient = pltpu.roll(fetched, 5, axis=0)
     sums = pair_acc[...]
     sums = sums[0:8] + sums[8:16] + sums[16:24]
     pair = (STIFFNESS / PAIR_SCALE) * (own_at * sums[4:5, :] - sums)
-    xs[0:3, :] = vel_ref[...]
+    for d in range(3):
+        xs[d : d + 1, :] = vel_ref[d]
     volume = vol_ref[...]
     force = drag_ref[...] * (fetched - xs[...]) - volume * gradient + pair
-    force_ref[...] = force[0:3]
+    for d in range(3):
+        force_ref[d] = force[d : d + 1]
+    force_copy = pltpu.make_async_copy(force_ref, force_out, out_ss.at[0])
+    force_copy.start()
     loads = jnp.where(row8 == 3, volume, force)
     load_send[...] = loads[0:4]
     for copy in load_copies:
         copy.start()
-
-    def edge_rows(fraction, rows):
-        d = fraction - (rows.astype(f32) + (0.5 - MARGIN)) * (1.0 / BX)
-        return jnp.exp2((d * d) * (-EDGE_RATE))
-
-    row24 = rows_iota((24, 1))
-    order_y = jnp.where(row24 < 16, row24 + 4, jnp.where(row24 < 20, row24 - 16, row24))
-
-    def all_edges(fx, fy):
-        bump_x = edge_rows(fx, row24)
-        bump_y = edge_rows(fy, order_y)
-        scale_x = 1.0 / jnp.sum(bump_x, axis=0, keepdims=True)
-        scale_y = 1.0 / jnp.sum(bump_y, axis=0, keepdims=True)
-        wx_ref[...] = bump_x * scale_x
-        wy_ref[...] = bump_y * scale_y
-
-    at_z = (lax.broadcasted_iota(jnp.int32, (1, BINS_THIRD_AXIS), 1).astype(f32) + 0.5) * (DEPTH_SCALE / BX)
-
-    def depth_rows(m):
-        def depth_step(i, carry):
-            r0 = pl.multiple_of(i * 64, 64)
-            block = cols[m, pl.ds(r0, 64), :]
-            d = block[:, 2:3] * (HEIGHT * DEPTH_SCALE) - at_z
-            wz[m, pl.ds(r0, 64), :] = jnp.exp2(block[:, 3:4] - d * d).astype(bf16)
-            return carry
-
-        lax.fori_loop(0, P_DEV // 64, depth_step, 0)
-
-    depth_rows(OWN)
-    all_edges(pos_send[0:1, :], pos_send[1:2, :])
 
     def spread_step(a, carry):
         plane = wx_ref[pl.ds(a + MARGIN, 1), :] * wy_ref[0:16, :]
@@ -319,14 +359,24 @@
         field_ref[c] = part.reshape(16, 16, BINS_THIRD_AXIS)
 
     def neighbour_depth(m, carry):
-        depth_rows(m)
+        depth_rows(2 * m)
+        depth_rows(2 * m + 1)
         return carry
 
-    lax.fori_loop(0, 8, neighbour_depth, 0)
+    lax.fori_loop(0, 4, neighbour_depth, 0)
 
     for copy in load_copies:
         copy.wait_recv()
-    for m, (dx, dy) in enumerate(STEPS):
+    out_copies = [force_copy]
+
+    def write_slabs(first, count, k):
+        part = pl.ds(first, count)
+        copy = pltpu.make_async_copy(field_ref.at[:, part], field_out.at[:, part], out_ss.at[k])
+        copy.start()
+        out_copies.append(copy)
+
+    for m in (3, 4, 0, 1, 2, 5, 6, 7):
+        dx, dy = STEPS[m]
         all_edges(pos_recv[m, 0:1, :], pos_recv[m, 1:2, :])
         loads_m = [load_recv[m, c : c + 1, :] * (FIELD_SCALE * present[m]) for c in range(4)]
         source_x = {-1: 20, 0: 4, 1: 0}[dx]
@@ -363,27 +413,61 @@
                     r0 = (c * count_x + a) * 4
                     field_ref[c, target_x + a, target_y : target_y + 4, :] += part[r0 : r0 + 4, :]
 
+        if m == 4:
+            write_slabs(4, 8, 1)
+        if m == 2:
+            write_slabs(0, 4, 2)
+    write_slabs(12, 4, 3)
+    for copy in out_copies:
+        copy.wait()
     for copy in pos_copies + req_copies + val_copies + load_copies:
         copy.wait_send()
+
+
+def publish(force_in, field_in, force_out, field_out, force_v, field_v, in_sems, out_sems):
+    pairs = [(force_in, force_v, force_out)]
+    for c in range(4):
+        for k in range(4):
+            part = pl.ds(4 * k, 4)
+            pairs.append((field_in.at[c, part], field_v.at[c, part], field_out.at[c, part]))
+    ins = [pltpu.make_async_copy(a, v, in_sems.at[i]) for i, (a, v, o) in enumerate(pairs)]
+    outs = [pltpu.make_async_copy(v, o, out_sems.at[i]) for i, (a, v, o) in enumerate(pairs)]
+    for copy in ins:
+        copy.start()
+    for first, second in zip(ins, outs):
+        first.wait()
+        second.start()
+    for copy in outs:
+        copy.wait()
 
 
 def body(fractions, velocity, drag_rate, volume, owner, element, coords, fluid):
     grid_x = lax.axis_size("gx")
     grid_y = lax.axis_size("gy")
-    nodes = fluid.reshape(E_DEV, 6, 512)
-    nothing = jnp.zeros((E_DEV, 1, 512), bf16)
-    table = jnp.concatenate([nodes[:, 0:3], nothing, nodes[:, 3:6], nothing], axis=1).reshape(256, 512)
-    vmem = pl.BlockSpec(memory_space=pltpu.VMEM)
+    table = jnp.transpose(fluid.reshape(E_DEV, 6, 512), (1, 0, 2)).reshape(E_DEV * 6, 512)
+    hbm = pl.BlockSpec(memory_space=pl.ANY)
     dma = pltpu.SemaphoreType.DMA((8,))
     force, field = pl.pallas_call(
         functools.partial(kernel, grid_x, grid_y),
         out_shape=(
-            jax.ShapeDtypeStruct((3, P_DEV), f32),
+            jax.ShapeDtypeStruct((3, 1, P_DEV), f32),
             jax.ShapeDtypeStruct((4, BX, BY, BINS_THIRD_AXIS), f32),
         ),
-        in_specs=[vmem] * 9,
-        out_specs=(vmem, vmem),
+        in_specs=[hbm] * 10,
+        out_specs=(hbm, hbm),
         scratch_shapes=[
+            pltpu.VMEM((3, 1, P_DEV), f32),
+            pltpu.VMEM((4, BX, BY, BINS_THIRD_AXIS), f32),
+            pltpu.VMEM((3, 1, P_DEV), f32),
+            pltpu.VMEM((3, 1, P_DEV), f32),
+            pltpu.VMEM((1, P_DEV), f32),
+            pltpu.VMEM((1, P_DEV), f32),
+            pltpu.VMEM((1, P_DEV), jnp.int32),
+            pltpu.VMEM((1, P_DEV), jnp.int32),
+            pltpu.VMEM((3, 1, P_DEV), jnp.int32),
+            pltpu.VMEM((6 * E_DEV, 512), bf16),
+            pltpu.VMEM((32, QUANT), bf16),
+            pltpu.VMEM((ROWS_Q, BINS_THIRD_AXIS), bf16),
             pltpu.VMEM((4, P_DEV), f32),
             pltpu.VMEM((8, 4, P_DEV), f32),
             pltpu.VMEM((4, 8, 128), f32),
@@ -394,7 +478,6 @@
             pltpu.VMEM((8, 4, P_DEV), f32),
             pltpu.VMEM((8, P_DEV), f32),
             pltpu.VMEM((9, P_DEV, ROWS_Q), bf16),
-            pltpu.VMEM((9, P_DEV, 8), f32),
             pltpu.VMEM((9, 32, P_DEV), bf16),
             pltpu.VMEM((ROWS_Q, P_DEV), bf16),
             pltpu.VMEM((8 * CAP, P_DEV), bf16),
@@ -409,22 +492,40 @@
             pltpu.VMEM((24, P_DEV), f32),
             pltpu.VMEM((8, P_DEV), f32),
         ]
-        + [dma] * 8,
+        + [pltpu.SemaphoreType.DMA((10,)), pltpu.SemaphoreType.DMA((4,))] + [dma] * 8,
         compiler_params=pltpu.CompilerParams(
-            collective_id=0, has_side_effects=True, vmem_limit_bytes=50 * 1024 * 1024
+            collective_id=0, has_side_effects=True, vmem_limit_bytes=60 * 1024 * 1024
         ),
         name="particle_step",
     )(
-        fractions.reshape(3, P_DEV),
-        velocity.reshape(3, P_DEV),
+        fractions.reshape(3, 1, P_DEV),
+        velocity.reshape(3, 1, P_DEV),
         drag_rate.reshape(1, P_DEV),
         volume.reshape(1, P_DEV),
         owner.reshape(1, P_DEV),
         element.reshape(1, P_DEV),
-        coords.reshape(3, P_DEV),
+        coords.reshape(3, 1, P_DEV),
         table,
         jnp.asarray(basis_pieces()),
+        jnp.asarray(depth_pieces()),
     )
+    force, field = pl.pallas_call(
+        publish,
+        out_shape=(
+            jax.ShapeDtypeStruct((3, 1, P_DEV), f32),
+            jax.ShapeDtypeStruct((4, BX, BY, BINS_THIRD_AXIS), f32),
+        ),
+        in_specs=[hbm] * 2,
+        out_specs=(hbm, hbm),
+        scratch_shapes=[
+            pltpu.VMEM((3, 1, P_DEV), f32),
+            pltpu.VMEM((4, BX, BY, BINS_THIRD_AXIS), f32),
+            pltpu.SemaphoreType.DMA((17,)),
+            pltpu.SemaphoreType.DMA((17,)),
+        ],
+        compiler_params=pltpu.CompilerParams(vmem_limit_bytes=60 * 1024 * 1024),
+        name="publish",
+    )(force, field)
     return force.reshape(1, 1, 3, P_DEV), field
 
 

time: 52.1 us -> 33.6 us (0.64)
  the two profiles are of different devices: /device:TPU:1 before, /device:TPU:0 now
where the time goes in v2:
time: 33.6 us; the launch traced here: 33.4 us
  Pallas kernels  32.7 us (97%)
  between operations  0.64 us (2%)
    pallas_call x1, Pallas kernels, body(): pl.pallas_call(functools.partial(kernel, grid_x, grid_y), out_shape=(jax....  30.1 us
    pallas_call x1, Pallas kernels, body(): pl.pallas_call(publish, out_shape=(jax.ShapeDtypeStruct((3, 1, P_DEV), f3...  2.6 us

profile of v2, /device:TPU:0, one launch (start us, length us, event | category | flops | bytes accessed | tf_op | source)
XLA Modules:
  0.0 33.4 jit_solution(3088067230688634716)
XLA Ops:
  0.6 30.1 %particle_step.1 = (f32[3,1,1024]{2,1,0:T(1,128)}, f32[4,16,16,512]{3,2,1,0:T(8,128)}) custom-call(f32[3,1,1024]{2,1,0:T(1,128)} %bitcast.16, f32[3,1,1024]{2,1,0:T(1,128)} %bitcast.17, f32[1,1024]{1,0:T(1,128)} %bitcast.19, f32[1,1024]{1,0:T(1,128)} %bitcast.20, s32[1,1024]{1,0:T(1,128)} %bitcast.21, s32[1,1024]{1,0:T(1,128)} %bitcast.22, ...), custom_call_target="tpu_custom_call" | custom-call | tf_op jit(solution)/shard_map/particle_step/pallas_call | solution.py:450
  30.8 2.6 %publish.1 = (f32[3,1,1024]{2,1,0:T(1,128)}, f32[4,16,16,512]{3,2,1,0:T(8,128)}) custom-call(f32[3,1,1024]{2,1,0:T(1,128)} %get-tuple-element.6.force_in, f32[4,16,16,512]{3,2,1,0:T(8,128)} %get-tuple-element.7.field_in), custom_call_target="tpu_custom_call" | custom-call | tf_op jit(solution)/shard_map/publish/pallas_call | solution.py:512

commit v3 on v2

--- a/solution.py
+++ b/solution.py
@@ -119,15 +119,36 @@
     me_y = lax.axis_index("gy")
     ids = []
     present = []
+    inside = []
     for dx, dy in STEPS:
         tx, ty = me_x + dx, me_y + dy
         ids.append((lax.rem(tx + grid_x, grid_x), lax.rem(ty + grid_y, grid_y)))
-        inside = (tx >= 0) & (tx < grid_x) & (ty >= 0) & (ty < grid_y)
-        present.append(jnp.where(inside, 1.0, 0.0).astype(f32))
+        within = (tx >= 0) & (tx < grid_x) & (ty >= 0) & (ty < grid_y)
+        inside.append(within)
+        present.append(jnp.where(within, 1.0, 0.0).astype(f32))
+    groups = ((None, (3, 4)), (me_x > 0, (0, 1, 2)), (me_x < grid_x - 1, (5, 6, 7)))
+
+    def guarded(condition, act):
+        if condition is None:
+            act()
+        else:
+            pl.when(condition)(act)
 
     barrier = pltpu.get_barrier_semaphore()
+    neighbours = jnp.int32(0)
     for n in range(8):
-        pl.semaphore_signal(barrier, inc=1, device_id=ids[n], device_id_type=MESH)
+        neighbours = neighbours + inside[n].astype(jnp.int32)
+
+        @pl.when(inside[n])
+        def _(n=n):
+            pl.semaphore_signal(barrier, inc=1, device_id=ids[n], device_id_type=MESH)
+
+        @pl.when(jnp.logical_not(inside[n]))
+        def _(n=n):
+            pos_recv[n] = jnp.zeros((4, P_DEV), f32)
+            load_recv[n] = jnp.zeros((4, P_DEV), f32)
+            req_recv[n] = jnp.zeros((8, 128), f32)
+            val_recv[n] = jnp.zeros((8, 128), f32)
 
     def remote(src, dst, ss, rs, n):
         return pltpu.make_async_remote_copy(
@@ -156,9 +177,15 @@
         pos_send[d : d + 1, :] = frac_ref[d]
     pos_send[3:4, :] = -LOG2E * jnp.log(total)
 
-    pl.semaphore_wait(barrier, 8)
-    for copy in pos_copies:
-        copy.start()
+    def start_all(copies):
+        for n in range(8):
+            pl.when(inside[n])(copies[n].start)
+
+    def arrive(copies, m):
+        pl.when(inside[m])(copies[7 - m].wait_recv)
+
+    pl.semaphore_wait(barrier, neighbours)
+    start_all(pos_copies)
 
     for copy in loads_in[1:]:
         copy.wait()
@@ -196,8 +223,7 @@
     )
     for j in range(4):
         req_send[j] = outgoing[0:8, 128 * j : 128 * j + 128]
-    for copy in req_copies:
-        copy.start()
+    start_all(req_copies)
 
     def interpolate(requests):
         slots = requests.shape[1]
@@ -241,9 +267,10 @@
         level = jnp.where(row == 0, h1, jnp.where(row == 1, h2, jnp.where(row == 2, h3, 0.0)))
         stack = jnp.concatenate([q1, q2, q1, q2, q3, q1, level, jnp.zeros_like(level)], axis=0)
         fq_t[m] = stack.T.astype(bf16)
+        packed = jnp.where(row < 5, q1, pltpu.roll(q3, 5, axis=0))
         if weight is not None:
-            q1, q2, q3 = q1 * weight, q2 * weight, q3 * weight
-        feat[m] = jnp.concatenate([q1, q2, q3, jnp.zeros_like(q1)], axis=0).astype(bf16)
+            packed, q2 = packed * weight, q2 * weight
+        feat[m] = jnp.concatenate([packed, q2], axis=0).astype(bf16)
         return where_at
 
     xs[0:4, :] = pos_send[...]
@@ -285,25 +312,18 @@
     all_edges(pos_send[0:1, :], pos_send[1:2, :])
     depth_rows(OWN)
 
-    def arrive(m):
-        pos_copies[7 - m].wait_recv()
-
-    def neighbour_features(m):
-        xs[0:4, :] = pos_recv[m]
-        features(m, STEPS[m][0], STEPS[m][1], present[m])
-
-    for m in (3, 4):
-        arrive(m)
-    for m in (3, 4):
-        neighbour_features(m)
-    pair_acc[...] += pair_block(3) + pair_block(4)
-    for m in (0, 1, 2, 5, 6, 7):
-        arrive(m)
-    for m in (0, 1, 2, 5, 6, 7):
-        neighbour_features(m)
-
-    for copy in req_copies:
-        copy.wait_recv()
+    def pair_group(members):
+        for m in members:
+            arrive(pos_copies, m)
+        for m in members:
+            xs[0:4, :] = pos_recv[m]
+            features(m, STEPS[m][0], STEPS[m][1], present[m])
+        pair_acc[...] += sum(pair_block(m) for m in members)
+
+    pair_group(groups[0][1])
+
+    for m in range(8):
+        arrive(req_copies, m)
     low_half = lax.broadcasted_iota(jnp.int32, (8, 128), 1) < CAP
     arrived = jnp.concatenate(
         [jnp.where(low_half, req_recv[2 * j + 1], req_recv[2 * j]) for j in range(4)], axis=1
@@ -311,17 +331,13 @@
     served = interpolate(arrived)
     for j in range(4):
         val_send[j] = served[:, 128 * j : 128 * j + 128]
-    for copy in val_copies:
-        copy.start()
-
-    def pair_step(m, carry):
-        pair_acc[...] += pair_block(m) + pair_block(m + 5)
-        return carry
-
-    lax.fori_loop(0, 3, pair_step, 0)
-
-    for copy in val_copies:
-        copy.wait_recv()
+    start_all(val_copies)
+
+    for condition, members in groups[1:]:
+        guarded(condition, functools.partial(pair_group, members))
+
+    for m in range(8):
+        arrive(val_copies, m)
     returned = jnp.concatenate(
         [jnp.where(low_half, val_recv[2 * j], val_recv[2 * j + 1]) for j in range(4)], axis=1
     )
@@ -330,8 +346,9 @@
     fetched = jnp.where(is_remote > 0.0, fetched, own_val[...])
     gradient = pltpu.roll(fetched, 5, axis=0)
     sums = pair_acc[...]
-    sums = sums[0:8] + sums[8:16] + sums[16:24]
-    pair = (STIFFNESS / PAIR_SCALE) * (own_at * sums[4:5, :] - sums)
+    count = sums[4:5, :]
+    sums = sums[0:8] + sums[8:16] + pltpu.roll(sums[0:8], 3, axis=0)
+    pair = (STIFFNESS / PAIR_SCALE) * (own_at * count - sums)
     for d in range(3):
         xs[d : d + 1, :] = vel_ref[d]
     volume = vol_ref[...]
@@ -342,8 +359,7 @@
     force_copy.start()
     loads = jnp.where(row8 == 3, volume, force)
     load_send[...] = loads[0:4]
-    for copy in load_copies:
-        copy.start()
+    start_all(load_copies)
 
     def spread_step(a, carry):
         plane = wx_ref[pl.ds(a + MARGIN, 1), :] * wy_ref[0:16, :]
@@ -358,15 +374,13 @@
         part = jnp.dot(spread_c[256 * c : 256 * c + 256, :], wz[OWN], preferred_element_type=f32)
         field_ref[c] = part.reshape(16, 16, BINS_THIRD_AXIS)
 
-    def neighbour_depth(m, carry):
-        depth_rows(2 * m)
-        depth_rows(2 * m + 1)
-        return carry
-
-    lax.fori_loop(0, 4, neighbour_depth, 0)
-
-    for copy in load_copies:
-        copy.wait_recv()
+    def depth_group(members):
+        for m in members:
+            depth_rows(m)
+
+    for condition, members in groups:
+        guarded(condition, functools.partial(depth_group, members))
+
     out_copies = [force_copy]
 
     def write_slabs(first, count, k):
@@ -375,10 +389,11 @@
         copy.start()
         out_copies.append(copy)
 
-    for m in (3, 4, 0, 1, 2, 5, 6, 7):
+    def margin(m):
         dx, dy = STEPS[m]
+        arrive(load_copies, m)
         all_edges(pos_recv[m, 0:1, :], pos_recv[m, 1:2, :])
-        loads_m = [load_recv[m, c : c + 1, :] * (FIELD_SCALE * present[m]) for c in range(4)]
+        loads_m = [load_recv[m, c : c + 1, :] * FIELD_SCALE for c in range(4)]
         source_x = {-1: 20, 0: 4, 1: 0}[dx]
         target_x = {-1: 0, 0: 0, 1: 12}[dx]
         count_x = 16 if dx == 0 else 4
@@ -413,15 +428,20 @@
                     r0 = (c * count_x + a) * 4
                     field_ref[c, target_x + a, target_y : target_y + 4, :] += part[r0 : r0 + 4, :]
 
-        if m == 4:
-            write_slabs(4, 8, 1)
-        if m == 2:
-            write_slabs(0, 4, 2)
-    write_slabs(12, 4, 3)
+
+    def margin_group(members):
+        for m in members:
+            margin(m)
+
+    for k, (first, count_x) in enumerate(((4, 8), (0, 4), (12, 4))):
+        condition, members = groups[k]
+        guarded(condition, functools.partial(margin_group, members))
+        write_slabs(first, count_x, 1 + k)
     for copy in out_copies:
         copy.wait()
-    for copy in pos_copies + req_copies + val_copies + load_copies:
-        copy.wait_send()
+    for copies in (pos_copies, req_copies, val_copies, load_copies):
+        for n in range(8):
+            pl.when(inside[n])(copies[n].wait_send)
 
 
 def publish(force_in, field_in, force_out, field_out, force_v, field_v, in_sems, out_sems):
@@ -478,12 +498,12 @@
             pltpu.VMEM((8, 4, P_DEV), f32),
             pltpu.VMEM((8, P_DEV), f32),
             pltpu.VMEM((9, P_DEV, ROWS_Q), bf16),
-            pltpu.VMEM((9, 32, P_DEV), bf16),
+            pltpu.VMEM((9, 16, P_DEV), bf16),
             pltpu.VMEM((ROWS_Q, P_DEV), bf16),
             pltpu.VMEM((8 * CAP, P_DEV), bf16),
             pltpu.VMEM((512, 512), bf16),
             pltpu.VMEM((8, P_DEV), f32),
-            pltpu.VMEM((32, P_DEV), f32),
+            pltpu.VMEM((16, P_DEV), f32),
             pltpu.VMEM((9, P_DEV, BINS_THIRD_AXIS), bf16),
             pltpu.VMEM((1024, P_DEV), bf16),
             pltpu.VMEM((256, P_DEV), bf16),

time: 33.6 us -> 29 us (0.86)
  the two profiles are of different devices: /device:TPU:0 before, /device:TPU:7 now
where the time goes in v3:
time: 29 us; the launch traced here: 28.7 us
  Pallas kernels  27.9 us (96%)
  between operations  0.8 us (3%)
    pallas_call x1, Pallas kernels, body(): pl.pallas_call(functools.partial(kernel, grid_x, grid_y), out_shape=(jax....  25.3 us
    pallas_call x1, Pallas kernels, body(): pl.pallas_call(publish, out_shape=(jax.ShapeDtypeStruct((3, 1, P_DEV), f3...  2.6 us

profile of v3, /device:TPU:7, one launch (start us, length us, event | category | flops | bytes accessed | tf_op | source)
XLA Modules:
  0.0 28.7 jit_solution(523889755153325869)
XLA Ops:
  0.6 25.3 %particle_step.1 = (f32[3,1,1024]{2,1,0:T(1,128)}, f32[4,16,16,512]{3,2,1,0:T(8,128)}) custom-call(f32[3,1,1024]{2,1,0:T(1,128)} %bitcast.16, f32[3,1,1024]{2,1,0:T(1,128)} %bitcast.17, f32[1,1024]{1,0:T(1,128)} %bitcast.19, f32[1,1024]{1,0:T(1,128)} %bitcast.20, s32[1,1024]{1,0:T(1,128)} %bitcast.21, s32[1,1024]{1,0:T(1,128)} %bitcast.22, ...), custom_call_target="tpu_custom_call" | custom-call | tf_op jit(solution)/shard_map/particle_step/pallas_call | solution.py:470
  25.9 2.6 %publish.1 = (f32[3,1,1024]{2,1,0:T(1,128)}, f32[4,16,16,512]{3,2,1,0:T(8,128)}) custom-call(f32[3,1,1024]{2,1,0:T(1,128)} %get-tuple-element.6.force_in, f32[4,16,16,512]{3,2,1,0:T(8,128)} %get-tuple-element.7.field_in), custom_call_target="tpu_custom_call" | custom-call | tf_op jit(solution)/shard_map/publish/pallas_call | solution.py:532

commit v4 on v3

--- a/solution.py
+++ b/solution.py
@@ -102,8 +102,8 @@
     force_ref, field_ref,
     frac_ref, vel_ref, drag_ref, vol_ref, owner_ref, element_ref, coords_ref, table_ref, basis_ref, depth_ref,
     pos_send, pos_recv, req_send, req_recv, val_send, val_recv, load_send, load_recv,
-    xs, fq_t, feat, fp, g_ref, weights, own_val, pair_acc, wz, spread_c, spread_e, wx_ref, wy_ref,
-    wx4, wy4,
+    xs, close, fq_t, feat, fp, g_ref, weights, own_val, pair_acc, wz, spread_c, spread_e, wx_ref, wy_ref,
+    wy4,
     in_ss, out_ss, pos_ss, pos_rs, req_ss, req_rs, val_ss, val_rs, load_ss, load_rs,
 ):
     inputs = (
@@ -282,10 +282,12 @@
     blank = jnp.zeros_like(p1)
     fp[...] = jnp.concatenate([p1, p1, p2, p2, p1, p3, blank, blank], axis=0).astype(bf16)
 
-    def pair_block(m):
+    def exponentials(m, turn):
         exponent = jnp.dot(fq_t[m], fp[...], preferred_element_type=f32)
-        closeness = jnp.exp2(exponent).astype(bf16)
-        return jnp.dot(feat[m], closeness, preferred_element_type=f32)
+        close[turn] = jnp.exp2(exponent).astype(bf16)
+
+    def pair_sums(m, turn):
+        return jnp.dot(feat[m], close[turn], preferred_element_type=f32)
 
     def edge_rows(fraction, rows):
         d = fraction - (rows.astype(f32) + (0.5 - MARGIN)) * (1.0 / BX)
@@ -294,33 +296,39 @@
     row24 = rows_iota((24, 1))
     order_y = jnp.where(row24 < 16, row24 + 4, jnp.where(row24 < 20, row24 - 16, row24))
 
-    def all_edges(fx, fy):
+    def all_edges(m, fx, fy):
         bump_x = edge_rows(fx, row24)
         bump_y = edge_rows(fy, order_y)
         scale_x = 1.0 / jnp.sum(bump_x, axis=0, keepdims=True)
         scale_y = 1.0 / jnp.sum(bump_y, axis=0, keepdims=True)
-        wx_ref[...] = bump_x * scale_x
-        wy_ref[...] = bump_y * scale_y
+        wx_ref[m] = bump_x * scale_x
+        wy_ref[m] = bump_y * scale_y
 
     def depth_rows(m):
         exponent = jnp.dot(fq_t[m], depth_ref[...], preferred_element_type=f32)
         wz[m] = jnp.exp2(exponent).astype(bf16)
 
-    pair_acc[...] = pair_block(OWN)
+    exponentials(OWN, 0)
     for half in range(2):
         own_val[:, 512 * half : 512 * half + 512] = interpolate(payload[:, 512 * half : 512 * half + 512])
-    all_edges(pos_send[0:1, :], pos_send[1:2, :])
+    all_edges(OWN, pos_send[0:1, :], pos_send[1:2, :])
     depth_rows(OWN)
 
-    def pair_group(members):
+    def pair_group(members, turns, before, turn_before, first):
         for m in members:
             arrive(pos_copies, m)
         for m in members:
             xs[0:4, :] = pos_recv[m]
             features(m, STEPS[m][0], STEPS[m][1], present[m])
-        pair_acc[...] += sum(pair_block(m) for m in members)
-
-    pair_group(groups[0][1])
+        acc = None if first else pair_acc[...]
+        for m, turn in zip(members, turns):
+            term = pair_sums(before, turn_before)
+            exponentials(m, turn)
+            acc = term if acc is None else acc + term
+            before, turn_before = m, turn
+        pair_acc[...] = acc
+
+    pair_group((3, 4), (1, 0), OWN, 0, True)
 
     for m in range(8):
         arrive(req_copies, m)
@@ -333,8 +341,12 @@
         val_send[j] = served[:, 128 * j : 128 * j + 128]
     start_all(val_copies)
 
-    for condition, members in groups[1:]:
-        guarded(condition, functools.partial(pair_group, members))
+    has_lower, has_upper = groups[1][0], groups[2][0]
+    guarded(has_lower, lambda: pair_group((0, 1, 2), (1, 0, 1), 4, 0, False))
+    block_before = jnp.where(has_lower, 2, 4)
+    turn_before = jnp.where(has_lower, 1, 0)
+    guarded(has_upper, lambda: pair_group((5, 6, 7), (2, 0, 1), block_before, turn_before, False))
+    pair_acc[...] += pair_sums(jnp.where(has_upper, 7, 2), 1)
 
     for m in range(8):
         arrive(val_copies, m)
@@ -362,7 +374,7 @@
     start_all(load_copies)
 
     def spread_step(a, carry):
-        plane = wx_ref[pl.ds(a + MARGIN, 1), :] * wy_ref[0:16, :]
+        plane = wx_ref[OWN, pl.ds(a + MARGIN, 1), :] * wy_ref[OWN, 0:16, :]
         for c in range(4):
             r0 = pl.multiple_of((c * 16 + a) * 16, 16)
             spread_c[pl.ds(r0, 16), :] = (plane * (load_send[c : c + 1, :] * FIELD_SCALE)).astype(bf16)
@@ -376,6 +388,7 @@
 
     def depth_group(members):
         for m in members:
+            all_edges(m, pos_recv[m, 0:1, :], pos_recv[m, 1:2, :])
             depth_rows(m)
 
     for condition, members in groups:
@@ -389,49 +402,57 @@
         copy.start()
         out_copies.append(copy)
 
-    def margin(m):
+    def spread_margin(m, k):
         dx, dy = STEPS[m]
-        arrive(load_copies, m)
-        all_edges(pos_recv[m, 0:1, :], pos_recv[m, 1:2, :])
         loads_m = [load_recv[m, c : c + 1, :] * FIELD_SCALE for c in range(4)]
         source_x = {-1: 20, 0: 4, 1: 0}[dx]
-        target_x = {-1: 0, 0: 0, 1: 12}[dx]
         count_x = 16 if dx == 0 else 4
         if dy == 0:
             for a in range(count_x):
-                plane = wx_ref[source_x + a : source_x + a + 1, :] * wy_ref[0:16, :]
+                plane = wx_ref[m, source_x + a : source_x + a + 1, :] * wy_ref[m, 0:16, :]
                 for c in range(4):
                     r0 = (c * count_x + a) * 16
-                    spread_e[r0 : r0 + 16, :] = (plane * loads_m[c]).astype(bf16)
-            part = jnp.dot(spread_e[...], wz[m], preferred_element_type=f32)
-            for c in range(4):
-                field_ref[c, target_x : target_x + 4] += part[64 * c : 64 * c + 64].reshape(4, 16, BINS_THIRD_AXIS)
+                    spread_e[k, r0 : r0 + 16, :] = (plane * loads_m[c]).astype(bf16)
         else:
             first = 20 if dy == -1 else 16
-            target_y = 0 if dy == -1 else 12
-            wy4[0:4, :] = wy_ref[first : first + 4, :]
-            wy4[4:8, :] = wy_ref[first : first + 4, :]
+            wy4[k, 0:4, :] = wy_ref[m, first : first + 4, :]
+            wy4[k, 4:8, :] = wy_ref[m, first : first + 4, :]
             top = rows_iota((8, 1)) < 4
             for a in range(0, count_x, 4):
                 planes = []
                 for pair_at in (a, a + 2):
                     s = source_x + pair_at
-                    planes.append(jnp.where(top, wx_ref[s : s + 1, :], wx_ref[s + 1 : s + 2, :]) * wy4[...])
+                    planes.append(
+                        jnp.where(top, wx_ref[m, s : s + 1, :], wx_ref[m, s + 1 : s + 2, :]) * wy4[k]
+                    )
                 plane = jnp.concatenate(planes, axis=0)
                 for c in range(4):
                     r0 = (c * count_x + a) * 4
-                    spread_e[r0 : r0 + 16, :] = (plane * loads_m[c]).astype(bf16)
-            used = 16 * count_x
-            part = jnp.dot(spread_e[0:used, :], wz[m], preferred_element_type=f32)
+                    spread_e[k, r0 : r0 + 16, :] = (plane * loads_m[c]).astype(bf16)
+
+    def add_margin(m, k):
+        dx, dy = STEPS[m]
+        target_x = {-1: 0, 0: 0, 1: 12}[dx]
+        count_x = 16 if dx == 0 else 4
+        used = 256 if dy == 0 else 16 * count_x
+        part = jnp.dot(spread_e[k, 0:used, :], wz[m], preferred_element_type=f32)
+        if dy == 0:
+            for c in range(4):
+                field_ref[c, target_x : target_x + 4] += part[64 * c : 64 * c + 64].reshape(4, 16, BINS_THIRD_AXIS)
+        else:
+            target_y = 0 if dy == -1 else 12
             for c in range(4):
                 for a in range(count_x):
                     r0 = (c * count_x + a) * 4
                     field_ref[c, target_x + a, target_y : target_y + 4, :] += part[r0 : r0 + 4, :]
 
-
     def margin_group(members):
         for m in members:
-            margin(m)
+            arrive(load_copies, m)
+        for k, m in enumerate(members):
+            spread_margin(m, k)
+        for k, m in enumerate(members):
+            add_margin(m, k)
 
     for k, (first, count_x) in enumerate(((4, 8), (0, 4), (12, 4))):
         condition, members = groups[k]
@@ -497,6 +518,7 @@
             pltpu.VMEM((4, P_DEV), f32),
             pltpu.VMEM((8, 4, P_DEV), f32),
             pltpu.VMEM((8, P_DEV), f32),
+            pltpu.VMEM((3, P_DEV, P_DEV), bf16),
             pltpu.VMEM((9, P_DEV, ROWS_Q), bf16),
             pltpu.VMEM((9, 16, P_DEV), bf16),
             pltpu.VMEM((ROWS_Q, P_DEV), bf16),
@@ -506,11 +528,10 @@
             pltpu.VMEM((16, P_DEV), f32),
             pltpu.VMEM((9, P_DEV, BINS_THIRD_AXIS), bf16),
             pltpu.VMEM((1024, P_DEV), bf16),
-            pltpu.VMEM((256, P_DEV), bf16),
-            pltpu.VMEM((24, P_DEV), f32),
-            pltpu.VMEM((24, P_DEV), f32),
-            pltpu.VMEM((24, P_DEV), f32),
-            pltpu.VMEM((8, P_DEV), f32),
+            pltpu.VMEM((3, 256, P_DEV), bf16),
+            pltpu.VMEM((9, 24, P_DEV), f32),
+            pltpu.VMEM((9, 24, P_DEV), f32),
+            pltpu.VMEM((3, 8, P_DEV), f32),
         ]
         + [pltpu.SemaphoreType.DMA((10,)), pltpu.SemaphoreType.DMA((4,))] + [dma] * 8,
         compiler_params=pltpu.CompilerParams(

time: 29 us -> 28 us (0.966)
  Pallas kernels: 27.9 us -> 27 us
    pallas_call x1, Pallas kernels: 25.3 us -> 24.4 us  [body(): pl.pallas_call(functools.partial(kernel, grid_x, grid_y), out_shape=(jax....]
where the time goes in v4:
time: 28 us; the launch traced here: 27.8 us
  Pallas kernels  27 us (96%)
  between operations  0.8 us (3%)
    pallas_call x1, Pallas kernels, body(): pl.pallas_call(functools.partial(kernel, grid_x, grid_y), out_shape=(jax....  24.4 us
    pallas_call x1, Pallas kernels, body(): pl.pallas_call(publish, out_shape=(jax.ShapeDtypeStruct((3, 1, P_DEV), f3...  2.6 us

profile of v4, /device:TPU:7, one launch (start us, length us, event | category | flops | bytes accessed | tf_op | source)
XLA Modules:
  0.0 27.8 jit_solution(2093838521432708939)
XLA Ops:
  0.6 24.4 %particle_step.1 = (f32[3,1,1024]{2,1,0:T(1,128)}, f32[4,16,16,512]{3,2,1,0:T(8,128)}) custom-call(f32[3,1,1024]{2,1,0:T(1,128)} %bitcast.16, f32[3,1,1024]{2,1,0:T(1,128)} %bitcast.17, f32[1,1024]{1,0:T(1,128)} %bitcast.19, f32[1,1024]{1,0:T(1,128)} %bitcast.20, s32[1,1024]{1,0:T(1,128)} %bitcast.21, s32[1,1024]{1,0:T(1,128)} %bitcast.22, ...), custom_call_target="tpu_custom_call" | custom-call | tf_op jit(solution)/shard_map/particle_step/pallas_call | solution.py:491
  25.0 2.6 %publish.1 = (f32[3,1,1024]{2,1,0:T(1,128)}, f32[4,16,16,512]{3,2,1,0:T(8,128)}) custom-call(f32[3,1,1024]{2,1,0:T(1,128)} %get-tuple-element.6.force_in, f32[4,16,16,512]{3,2,1,0:T(8,128)} %get-tuple-element.7.field_in), custom_call_target="tpu_custom_call" | custom-call | tf_op jit(solution)/shard_map/publish/pallas_call | solution.py:553

commit v5 on v4

--- a/solution.py
+++ b/solution.py
@@ -102,7 +102,7 @@
     force_ref, field_ref,
     frac_ref, vel_ref, drag_ref, vol_ref, owner_ref, element_ref, coords_ref, table_ref, basis_ref, depth_ref,
     pos_send, pos_recv, req_send, req_recv, val_send, val_recv, load_send, load_recv,
-    xs, close, fq_t, feat, fp, g_ref, weights, own_val, pair_acc, wz, spread_c, spread_e, wx_ref, wy_ref,
+    xs, scaled, close, fq_t, feat, fp, g_ref, weights, own_val, pair_acc, wz, spread_c, spread_e, wx_ref, wy_ref,
     wy4,
     in_ss, out_ss, pos_ss, pos_rs, req_ss, req_rs, val_ss, val_rs, load_ss, load_rs,
 ):
@@ -178,7 +178,7 @@
     pos_send[3:4, :] = -LOG2E * jnp.log(total)
 
     def start_all(copies):
-        for n in range(8):
+        for n in (3, 4, 0, 1, 2, 5, 6, 7):
             pl.when(inside[n])(copies[n].start)
 
     def arrive(copies, m):
@@ -223,9 +223,8 @@
     )
     for j in range(4):
         req_send[j] = outgoing[0:8, 128 * j : 128 * j + 128]
-    start_all(req_copies)
-
-    def interpolate(requests):
+
+    def interpolate(requests, k):
         slots = requests.shape[1]
         levels = rows_iota((QUANT, 1)).astype(f32)
         factors = []
@@ -240,8 +239,8 @@
                     [plane[b : b + 1, :] * factors[2], plane[b + 1 : b + 2, :] * factors[2]], axis=0
                 )
                 at = 64 * a + 8 * b
-                weights[at : at + 16, :] = pair.astype(bf16)
-        projected = jnp.dot(table_ref[...], weights[...], preferred_element_type=f32)
+                weights[k, at : at + 16, :] = pair.astype(bf16)
+        projected = jnp.dot(table_ref[...], weights[k], preferred_element_type=f32)
         mine = requests[0:1, :] == rows_iota((E_DEV, 1)).astype(f32)
         values = [
             jnp.sum(jnp.where(mine, projected[E_DEV * k : E_DEV * k + E_DEV, :], 0.0), axis=0, keepdims=True)
@@ -309,8 +308,9 @@
         wz[m] = jnp.exp2(exponent).astype(bf16)
 
     exponentials(OWN, 0)
+    start_all(req_copies)
     for half in range(2):
-        own_val[:, 512 * half : 512 * half + 512] = interpolate(payload[:, 512 * half : 512 * half + 512])
+        own_val[:, 512 * half : 512 * half + 512] = interpolate(payload[:, 512 * half : 512 * half + 512], half)
     all_edges(OWN, pos_send[0:1, :], pos_send[1:2, :])
     depth_rows(OWN)
 
@@ -336,7 +336,7 @@
     arrived = jnp.concatenate(
         [jnp.where(low_half, req_recv[2 * j + 1], req_recv[2 * j]) for j in range(4)], axis=1
     )
-    served = interpolate(arrived)
+    served = interpolate(arrived, 2)
     for j in range(4):
         val_send[j] = served[:, 128 * j : 128 * j + 128]
     start_all(val_copies)
@@ -373,11 +373,13 @@
     load_send[...] = loads[0:4]
     start_all(load_copies)
 
+    scaled[...] = load_send[...] * FIELD_SCALE
+
     def spread_step(a, carry):
         plane = wx_ref[OWN, pl.ds(a + MARGIN, 1), :] * wy_ref[OWN, 0:16, :]
         for c in range(4):
             r0 = pl.multiple_of((c * 16 + a) * 16, 16)
-            spread_c[pl.ds(r0, 16), :] = (plane * (load_send[c : c + 1, :] * FIELD_SCALE)).astype(bf16)
+            spread_c[pl.ds(r0, 16), :] = (plane * scaled[c : c + 1, :]).astype(bf16)
         return carry
 
     lax.fori_loop(0, 16, spread_step, 0)
@@ -430,29 +432,31 @@
                     r0 = (c * count_x + a) * 4
                     spread_e[k, r0 : r0 + 16, :] = (plane * loads_m[c]).astype(bf16)
 
-    def add_margin(m, k):
+    def product(m, k):
+        used = 256 if STEPS[m][1] == 0 or STEPS[m][0] == 0 else 64
+        return jnp.dot(spread_e[k, 0:used, :], wz[m], preferred_element_type=f32)
+
+    def add_part(m, part, c):
         dx, dy = STEPS[m]
         target_x = {-1: 0, 0: 0, 1: 12}[dx]
         count_x = 16 if dx == 0 else 4
-        used = 256 if dy == 0 else 16 * count_x
-        part = jnp.dot(spread_e[k, 0:used, :], wz[m], preferred_element_type=f32)
         if dy == 0:
-            for c in range(4):
-                field_ref[c, target_x : target_x + 4] += part[64 * c : 64 * c + 64].reshape(4, 16, BINS_THIRD_AXIS)
+            field_ref[c, target_x : target_x + 4] += part[64 * c : 64 * c + 64].reshape(4, 16, BINS_THIRD_AXIS)
         else:
             target_y = 0 if dy == -1 else 12
-            for c in range(4):
-                for a in range(count_x):
-                    r0 = (c * count_x + a) * 4
-                    field_ref[c, target_x + a, target_y : target_y + 4, :] += part[r0 : r0 + 4, :]
+            for a in range(count_x):
+                r0 = (c * count_x + a) * 4
+                field_ref[c, target_x + a, target_y : target_y + 4, :] += part[r0 : r0 + 4, :]
 
     def margin_group(members):
         for m in members:
             arrive(load_copies, m)
         for k, m in enumerate(members):
             spread_margin(m, k)
-        for k, m in enumerate(members):
-            add_margin(m, k)
+        parts = [product(m, k) for k, m in enumerate(members)]
+        for c in range(4):
+            for m, part in zip(members, parts):
+                add_part(m, part, c)
 
     for k, (first, count_x) in enumerate(((4, 8), (0, 4), (12, 4))):
         condition, members = groups[k]
@@ -468,8 +472,8 @@
 def publish(force_in, field_in, force_out, field_out, force_v, field_v, in_sems, out_sems):
     pairs = [(force_in, force_v, force_out)]
     for c in range(4):
-        for k in range(4):
-            part = pl.ds(4 * k, 4)
+        for k in range(2):
+            part = pl.ds(8 * k, 8)
             pairs.append((field_in.at[c, part], field_v.at[c, part], field_out.at[c, part]))
     ins = [pltpu.make_async_copy(a, v, in_sems.at[i]) for i, (a, v, o) in enumerate(pairs)]
     outs = [pltpu.make_async_copy(v, o, out_sems.at[i]) for i, (a, v, o) in enumerate(pairs)]
@@ -518,12 +522,13 @@
             pltpu.VMEM((4, P_DEV), f32),
             pltpu.VMEM((8, 4, P_DEV), f32),
             pltpu.VMEM((8, P_DEV), f32),
+            pltpu.VMEM((4, P_DEV), f32),
             pltpu.VMEM((3, P_DEV, P_DEV), bf16),
             pltpu.VMEM((9, P_DEV, ROWS_Q), bf16),
             pltpu.VMEM((9, 16, P_DEV), bf16),
             pltpu.VMEM((ROWS_Q, P_DEV), bf16),
             pltpu.VMEM((8 * CAP, P_DEV), bf16),
-            pltpu.VMEM((512, 512), bf16),
+            pltpu.VMEM((3, 512, 512), bf16),
             pltpu.VMEM((8, P_DEV), f32),
             pltpu.VMEM((16, P_DEV), f32),
             pltpu.VMEM((9, P_DEV, BINS_THIRD_AXIS), bf16),

time: 28 us -> 27.9 us (level)
  no operation moved by 1% of the time
where the time goes in v5:
time: 27.9 us; the launch traced here: 27.7 us
  Pallas kernels  26.9 us (96%)
  between operations  0.8 us (3%)
    pallas_call x1, Pallas kernels, body(): pl.pallas_call(functools.partial(kernel, grid_x, grid_y), out_shape=(jax....  24.3 us
    pallas_call x1, Pallas kernels, body(): pl.pallas_call(publish, out_shape=(jax.ShapeDtypeStruct((3, 1, P_DEV), f3...  2.57 us

profile of v5, /device:TPU:7, one launch (start us, length us, event | category | flops | bytes accessed | tf_op | source)
XLA Modules:
  0.0 27.7 jit_solution(17638897321400041332)
XLA Ops:
  0.6 24.3 %particle_step.1 = (f32[3,1,1024]{2,1,0:T(1,128)}, f32[4,16,16,512]{3,2,1,0:T(8,128)}) custom-call(f32[3,1,1024]{2,1,0:T(1,128)} %bitcast.16, f32[3,1,1024]{2,1,0:T(1,128)} %bitcast.17, f32[1,1024]{1,0:T(1,128)} %bitcast.19, f32[1,1024]{1,0:T(1,128)} %bitcast.20, s32[1,1024]{1,0:T(1,128)} %bitcast.21, s32[1,1024]{1,0:T(1,128)} %bitcast.22, ...), custom_call_target="tpu_custom_call" | custom-call | tf_op jit(solution)/shard_map/particle_step/pallas_call | solution.py:495
  24.9 2.6 %publish.1 = (f32[3,1,1024]{2,1,0:T(1,128)}, f32[4,16,16,512]{3,2,1,0:T(8,128)}) custom-call(f32[3,1,1024]{2,1,0:T(1,128)} %get-tuple-element.6.force_in, f32[4,16,16,512]{3,2,1,0:T(8,128)} %get-tuple-element.7.field_in), custom_call_target="tpu_custom_call" | custom-call | tf_op jit(solution)/shard_map/publish/pallas_call | solution.py:558
